TPU v7x, 512 devices: a whole 4x8x8 slice. The times are simulated.
512 devices in a mesh: exp: 16 (over x, z_lo), rep: 4 (over z_hi, core), tk: 8 (over y).
Axes of the slice: x: 4, y: 8, z: 8 (z_hi: 2, z_lo: 4; z = z_hi * 4 + z_lo), core: 2. Of those that a mesh axis runs over, the one named last changes fastest.
Arguments:
- hidden_input_rows: bfloat16 [8192, 2048], P(('exp', 'rep', 'tk')), may hold values from -6 to 6
- queries: bfloat16 [8192, 2048], P(('exp', 'rep', 'tk')), may hold values from -300 to 300
- new_keys: bfloat16 [8192, 512], P(('exp', 'rep', 'tk')), may hold values from -8 to 8
- new_values: bfloat16 [8192, 512], P(('exp', 'rep', 'tk')), may hold values from -6 to 6
- cache_keys: bfloat16 [8192, 64, 512], P(('exp', 'rep', 'tk')), may hold values from -8 to 8
- cache_values: bfloat16 [8192, 64, 512], P(('exp', 'rep', 'tk')), may hold values from -6 to 6
- cache_lengths: int32 [8192], P(('exp', 'rep', 'tk')), may hold values from 1 to 64, as said below
- moe_gain: bfloat16 [2048], replicated, may hold values from 0.099609375 to 1.8984375
- expert_ids: int32 [8192, 8], P(('exp', 'rep', 'tk')), may hold values from 0 to 127, as said below
- routing_weights: bfloat16 [8192, 8], P(('exp', 'rep', 'tk')), may hold values from 0.049804688 to 1
- expert_gate: bfloat16 [128, 2048, 768], P(('exp', 'tk'), None, 'rep'), may hold values from -0.125 to 0.125
- expert_up: bfloat16 [128, 2048, 768], P(('exp', 'tk'), None, 'rep'), may hold values from -0.125 to 0.125
- expert_down: bfloat16 [128, 2048, 768], P(('exp', 'tk'), None, 'rep'), may hold values from -0.21875 to 0.21875
- prev_hidden: bfloat16 [8192, 2048], P(('exp', 'rep', 'tk')), may hold values from -6 to 6
- talker_gain: bfloat16 [2048], replicated, may hold values from 0.099609375 to 1.8984375
- talker_proj: bfloat16 [2048, 1024], P(None, 'tk'), may hold values from -0.125 to 0.125
Outputs:
- layer_out: bfloat16 [8192, 2048], P(('exp', 'rep', 'tk'))
- talker_in: bfloat16 [8192, 1024], P(('exp', 'rep'), 'tk')
Inputs may be any that keep to these rules, and one draw needn't show every extreme that they name: `cache_lengths`: the first row of every device has all 64 positions valid. `expert_ids`: the 8 experts of a row differ. The rows of one device name no expert more than 2 times; some expert is named exactly 2 times by the rows of every device.
All inputs are finite; a program needn't handle non-finite values.
Results may differ from a plain program's by a relative error of at most 0.015.
Values may be sent and summed in bfloat16 or wider, within the bound.
No kernel may reach another device: no remote copies, remote signals or barrier semaphores. Data moves between devices by JAX's collectives and lax.ppermute only.
A program may use at most 64 MiB of HBM per device.

v0:
```python
import jax
import jax.numpy as jnp
from jax import lax
from jax.sharding import PartitionSpec as P

HD = 128
KVH = 4


def normalize(values, gain):
    wide = values.astype(jnp.float32)
    return (
        wide
        * lax.rsqrt(jnp.mean(wide * wide, axis=-1, keepdims=True) + 1e-06)
        * gain.astype(jnp.float32)
    )


def attend(queries, new_keys, new_values, cache_keys, cache_values, cache_lengths):
    count = queries.shape[0]
    span = cache_keys.shape[1]
    query_vector = queries.reshape(count, KVH, -1, HD)
    keys = cache_keys.reshape(count, span, KVH, HD)
    values = cache_values.reshape(count, span, KVH, HD)
    newest_key_row = new_keys.reshape(count, KVH, HD)
    fresh_value = new_values.reshape(count, KVH, HD)
    attention_scale = HD ** (-0.5)
    cached = (
        jnp.einsum("bkgd,bjkd->bkgj", query_vector, keys, preferred_element_type=jnp.float32)
        * attention_scale
    )
    local_owned = (
        jnp.einsum(
            "crno,cro->crn", query_vector, newest_key_row, preferred_element_type=jnp.float32
        )
        * attention_scale
    )
    valid = (jnp.arange(span, dtype=jnp.int32)[None, :] < cache_lengths[:, None])[:, None, None, :]
    top = jnp.maximum(jnp.max(jnp.where(valid, cached, -jnp.inf), axis=-1), local_owned)
    weight_cache = jnp.where(valid, jnp.exp(cached - top[..., None]), 0.0)
    owned_weight = jnp.exp(local_owned - top)
    total = jnp.sum(weight_cache, axis=-1) + owned_weight
    prob_cache = (weight_cache / total[..., None]).astype(jnp.bfloat16)
    prob_own = (owned_weight / total).astype(jnp.bfloat16)
    mixed = jnp.einsum("bkgj,bjkd->bkgd", prob_cache, values, preferred_element_type=jnp.float32)
    mixed = (
        mixed
        + prob_own.astype(jnp.float32)[..., None] * fresh_value.astype(jnp.float32)[:, :, None, :]
    )
    return mixed.reshape(count, -1)


def dense_route(expert_ids, routing_weights, experts):
    hits = expert_ids[:, :, None] == jnp.arange(experts, dtype=jnp.int32)[None, None, :]
    spread = jnp.where(hits, routing_weights.astype(jnp.float32)[:, :, None], 0.0)
    return jnp.sum(spread, axis=1).astype(jnp.bfloat16)


def slot_table(route, capacity):
    member = route > 0
    ranking = jnp.cumsum(member.astype(jnp.int32), axis=-2) - 1
    return jnp.logical_and(
        member[..., None], ranking[..., None] == jnp.arange(capacity, dtype=jnp.int32)
    )


def expert_apply(slots, gate, raise_weight, down):
    width = slots.shape[-1]
    flat = slots.reshape(-1, width)
    gated = jnp.dot(flat, gate, preferred_element_type=jnp.float32)
    raised = jnp.dot(flat, raise_weight, preferred_element_type=jnp.float32)
    active = (jax.nn.silu(gated) * raised).astype(jnp.bfloat16)
    output = lax.dot_general(
        active, down, (((1,), (1,)), ((), ())), preferred_element_type=jnp.float32
    )
    return output.astype(jnp.bfloat16).reshape(slots.shape)


def per_device(
    hidden_input_rows,
    queries,
    new_keys,
    new_values,
    cache_keys,
    cache_values,
    cache_lengths,
    moe_gain,
    expert_ids,
    routing_weights,
    expert_gate,
    expert_up,
    expert_down,
    prev_hidden,
    talker_gain,
    talker_proj,
):
    count = hidden_input_rows.shape[0]
    width = hidden_input_rows.shape[1]
    experts = lax.axis_size("exp") * lax.axis_size("tk")
    replicas = lax.axis_size("rep")
    chosen_count = expert_ids.shape[1]
    capacity = min(count, max(2, 2 * count * chosen_count // experts))
    attended = attend(queries, new_keys, new_values, cache_keys, cache_values, cache_lengths)
    residual = hidden_input_rows.astype(jnp.float32) + attended
    moe_in = normalize(residual, moe_gain).astype(jnp.bfloat16)
    route = dense_route(expert_ids, routing_weights, experts)
    gate_local = expert_gate[0]
    up_local = expert_up[0]
    down_local = expert_down[0]
    group_input_rows, group_route = (
        lax.all_gather(moe_in, "rep", axis=0, tiled=True),
        lax.all_gather(route, "rep", axis=0, tiled=True),
    )
    group_input_rows = group_input_rows.reshape(replicas, count, width)
    group_route = group_route.reshape(replicas, count, experts)
    table = slot_table(group_route, capacity)
    outgoing = jnp.einsum(
        "rnec,rnd->ercd",
        table.astype(jnp.bfloat16),
        group_input_rows,
        preferred_element_type=jnp.float32,
    )
    outgoing = outgoing.astype(jnp.bfloat16).reshape(experts, replicas * capacity, width)
    computed = expert_apply(
        lax.all_to_all(outgoing, ("exp", "tk"), split_axis=0, concat_axis=0, tiled=True),
        gate_local,
        up_local,
        down_local,
    )
    returned = lax.all_to_all(computed, ("exp", "tk"), split_axis=0, concat_axis=0, tiled=True)
    weighted = jnp.where(table, group_route[..., None], jnp.zeros((), jnp.bfloat16))
    partial_rows = jnp.einsum(
        "rnec,ercd->rnd",
        weighted,
        returned.reshape(experts, replicas, capacity, width),
        preferred_element_type=jnp.float32,
    )
    combined = lax.psum_scatter(
        partial_rows.reshape(replicas * count, width).astype(jnp.bfloat16),
        "rep",
        scatter_dimension=0,
        tiled=True,
    ).astype(jnp.float32)
    layer_out = (residual + combined).astype(jnp.bfloat16)
    talker_rows = normalize(prev_hidden, talker_gain).astype(jnp.bfloat16)
    talker_in = jnp.dot(
        lax.all_gather(talker_rows, "tk", axis=0, tiled=True),
        talker_proj,
        preferred_element_type=jnp.float32,
    ).astype(jnp.bfloat16)
    return (layer_out, talker_in)


def solution(mesh):
    placed = (
        P(("exp", "rep", "tk"), None),
        P(("exp", "rep", "tk"), None),
        P(("exp", "rep", "tk"), None),
        P(("exp", "rep", "tk"), None),
        P(("exp", "rep", "tk"), None, None),
        P(("exp", "rep", "tk"), None, None),
        P(("exp", "rep", "tk")),
        P(),
        P(("exp", "rep", "tk"), None),
        P(("exp", "rep", "tk"), None),
        P(("exp", "tk"), None, "rep"),
        P(("exp", "tk"), None, "rep"),
        P(("exp", "tk"), None, "rep"),
        P(("exp", "rep", "tk"), None),
        P(),
        P(None, "tk"),
    )
    return jax.shard_map(
        per_device,
        mesh=mesh,
        in_specs=placed,
        out_specs=(P(("exp", "rep", "tk"), None), P(("exp", "rep"), "tk")),
        check_vma=False,
    )
```

profile of v0, /device:TPU:1, one launch (start us, length us, event | category | flops | bytes accessed | tf_op | source)
XLA Modules:
  0.0 332.7 jit_solution(4334787898838924920)
XLA Ops:
  7.2 0.8 iota_compare_fusion.2
  8.0 0.9 reshape.105
  8.9 0.7 reshape.122
  9.6 0.2 fusion.50
  9.8 2.0 select_reduce_fusion
  11.8 0.3 fusion.29
  12.2 0.7 reshape.116
  12.9 0.5 convolution_add_fusion
  13.5 0.1 multiply_reduce_fusion
  13.6 0.1 multiply_convert_fusion
  13.7 16.4 %all_gather.10 = bf16[64,2048]{1,0:T(8,128)(2,1)S(1)} all-gather(bf16[16,2048]{1,0:T(8,128)(2,1)S(1)} %multiply_convert_fusion), channel_id=1, replica_groups=mesh['exp'=16,'rep'=4,'tk'=8] {'rep'}, dimensions={0}, use_global_device_ids=true | all-gather | bytes 327680 | tf_op jit(solution)/shard_map/all_gather | solution.py:111
  30.1 0.1 copy.31
  30.2 0.1 copy.32
  30.3 0.1 select_reduce_fusion.1
  30.4 9.0 %all_gather.9 = bf16[64,128]{1,0:T(8,128)(2,1)S(1)} all-gather(bf16[16,128]{1,0:T(8,128)(2,1)S(1)} %select_reduce_fusion.1), channel_id=1, replica_groups=mesh['exp'=16,'rep'=4,'tk'=8] {'rep'}, dimensions={0}, use_global_device_ids=true | all-gather | bytes 20480 | tf_op jit(solution)/shard_map/all_gather | solution.py:112
  39.5 3.2 convolution_convert_fusion
  42.7 6.7 %copy.33 = bf16[128,8,2048]{2,1,0:T(8,128)(2,1)} copy(bf16[128,8,2048]{0,2,1:T(8,128)(2,1)} %bitcast.66) | data formatting | bytes 8388608 | tf_op jit(solution)/shard_map/reshape | solution.py:123
  49.4 111.2 %all_to_all.10 = bf16[128,8,2048]{2,1,0:T(8,128)(2,1)S(1)} all-to-all(bf16[128,8,2048]{2,1,0:T(8,128)(2,1)} %copy.33), channel_id=1, replica_groups=mesh['exp'=16,'rep'=4,'tk'=8] {'exp','tk'}, dimensions={0} | all-to-all | bytes 8388608 | tf_op jit(solution)/shard_map/all_to_all | solution.py:125
  160.6 2.0 copy-done.1
  162.6 2.5 fusion.2
  165.1 7.3 %convert_bitcast_fusion = bf16[128,8,2048]{2,1,0:T(8,128)(2,1)} fusion(bf16[1,2048,192]{1,2,0:T(8,128)(2,1)S(1)} %copy-done.10, bf16[128,8,2048]{2,1,0:T(8,128)(2,1)} %copy-done.1, bf16[1,2048,192]{1,2,0:T(8,128)(2,1)} %param.27, f32[1024,192]{0,1:T(8,128)} %fusion.2), kind=kOutput, calls=%fused_computation.4 | convolution fusion | flops 1613889536 | bytes 10747904 | tf_op jit(solution)/shard_map/dot_general | solution.py:73
  172.4 9.5 %all-to-all-start.1 = ((bf16[128,8,2048]{2,1,0:T(8,128)(2,1)}), bf16[128,8,2048]{2,1,0:T(8,128)(2,1)}, u32[]{:S(2)}, u32[]{:S(2)}) async-start(bf16[128,8,2048]{2,1,0:T(8,128)(2,1)} %convert_bitcast_fusion), calls=%async_computation.1 | async-start | bytes 8388608 | tf_op jit(solution)/shard_map/all_to_all | solution.py:130
  181.9 0.2 reduce-scatter.2.cloned.1.call-start
  182.2 0.1 fusion.26
  182.3 96.4 %all-to-all-done.1 = bf16[128,8,2048]{2,1,0:T(8,128)(2,1)} async-done(((bf16[128,8,2048]{2,1,0:T(8,128)(2,1)}), bf16[128,8,2048]{2,1,0:T(8,128)(2,1)}, u32[]{:S(2)}, u32[]{:S(2)}) %all-to-all-start.1) | async-done | bytes 4194336 | tf_op jit(solution)/shard_map/all_to_all | solution.py:130
  278.8 4.5 %copy.34 = bf16[128,8,2048]{2,0,1:T(8,128)(2,1)S(1)} copy(bf16[128,8,2048]{2,1,0:T(8,128)(2,1)} %all-to-all-done.1) | data formatting | bytes 8388608 | tf_op jit(solution)/shard_map/all_to_all | solution.py:130
  283.3 1.4 fusion.4
  284.6 0.1 fusion.28
  284.7 19.9 %all_gather.11 = bf16[128,2048]{1,0:T(8,128)(2,1)S(1)} all-gather(bf16[16,2048]{1,0:T(8,128)(2,1)S(1)} %fusion.28), channel_id=1, replica_groups=mesh['exp'=16,'rep'=4,'tk'=8] {'tk'}, dimensions={0}, use_global_device_ids=true | all-gather | bytes 589824 | tf_op jit(solution)/shard_map/all_gather | solution.py:147
  304.7 0.9 convolution_convert_fusion.1
  305.6 18.8 %reduce-scatter.2.cloned.1.call-done = bf16[16,2048]{1,0:T(8,128)(2,1)} async-done(((bf16[64,2048]{1,0:T(8,128)(2,1)}), bf16[16,2048]{1,0:T(8,128)(2,1)}) %reduce-scatter.2.cloned.1.call-update) | async-done | bytes 65552 | tf_op jit(solution)/shard_map/reduce_scatter | solution.py:138
  324.3 1.5 add_convert_fusion
  (32 shorter events, 0.3 us)
Async XLA Ops:
  7.2 5.8 %copy-start = (bf16[16,64,512]{2,1,0:T(8,128)(2,1)S(1)}, bf16[16,64,512]{2,1,0:T(8,128)(2,1)}, u32[]{:S(2)}) copy-start(bf16[16,64,512]{2,1,0:T(8,128)(2,1)} %param.21) | copy-start | bytes 3145732
  7.2 6.3 %copy-start.2 = (bf16[16,2048]{1,0:T(8,128)(2,1)S(1)}, bf16[16,2048]{1,0:T(8,128)(2,1)}, u32[]{:S(2)}) copy-start(bf16[16,2048]{1,0:T(8,128)(2,1)} %param.16) | copy-start | bytes 196612
  7.2 6.4 %copy-start.5 = (bf16[2048]{0:T(1024)(128)(2,1)S(1)}, bf16[2048]{0:T(1024)(128)(2,1)}, u32[]{:S(2)}) copy-start(bf16[2048]{0:T(1024)(128)(2,1)} %param.23) | copy-start | bytes 12292
  7.2 22.9 %copy-start.6 = (s32[16,8]{0,1:T(8,128)S(1)}, s32[16,8]{0,1:T(8,128)}, u32[]{:S(2)}) copy-start(s32[16,8]{0,1:T(8,128)} %param.24) | copy-start | bytes 1540
  7.2 23.0 %copy-start.8 = (bf16[16,8]{0,1:T(8,128)(2,1)S(1)}, bf16[16,8]{0,1:T(8,128)(2,1)}, u32[]{:S(2)}) copy-start(bf16[16,8]{0,1:T(8,128)(2,1)} %param.25) | copy-start | bytes 772
  49.4 113.2 %copy-start.9 = (bf16[1,2048,192]{1,2,0:T(8,128)(2,1)S(1)}, bf16[1,2048,192]{1,2,0:T(8,128)(2,1)}, u32[]{:S(2)}) copy-start(bf16[1,2048,192]{1,2,0:T(8,128)(2,1)} %param.26) | copy-start | bytes 2359300
  160.6 2.0 copy-start.1
  162.6 2.5 copy-start.10
  172.4 9.8 %copy-start.7 = (bf16[2048]{0:T(1024)(128)(2,1)S(1)}, bf16[2048]{0:T(1024)(128)(2,1)}, u32[]{:S(2)}) copy-start(bf16[2048]{0:T(1024)(128)(2,1)} %param.30) | copy-start | bytes 12292
  172.4 9.8 %copy-start.4 = (bf16[16,2048]{1,0:T(8,128)(2,1)S(1)}, bf16[16,2048]{1,0:T(8,128)(2,1)}, u32[]{:S(2)}) copy-start(bf16[16,2048]{1,0:T(8,128)(2,1)} %param.29) | copy-start | bytes 196612
  172.4 106.4 %all-to-all-start.1 = ((bf16[128,8,2048]{2,1,0:T(8,128)(2,1)}), bf16[128,8,2048]{2,1,0:T(8,128)(2,1)}, u32[]{:S(2)}, u32[]{:S(2)}) async-start(bf16[128,8,2048]{2,1,0:T(8,128)(2,1)} %convert_bitcast_fusion), calls=%async_computation.1 | async-start | bytes 8388608 | tf_op jit(solution)/shard_map/all_to_all | solution.py:130
  181.9 142.4 %reduce-scatter.2.cloned.1.call-start = ((), (), s32[]{:S(2)}) async-start(), calls=%async_computation.3 | async-start | bytes 327680 | tf_op jit(solution)/shard_map/reduce_scatter | solution.py:138
  283.3 21.4 %copy-start.3 = (bf16[2048,128]{1,0:T(8,128)(2,1)S(1)}, bf16[2048,128]{1,0:T(8,128)(2,1)}, u32[]{:S(2)}) copy-start(bf16[2048,128]{1,0:T(8,128)(2,1)} %param.31) | copy-start | bytes 1572868
Sparse Core Ops, SparseCore 0:
  284.8 39.5 reduce-scatter.1
where the time goes:
time: 333 us
  blocking collectives  157 us (47%)
  waiting for transfers between devices  115 us (35%)
  matrix products  17.9 us (5%)
  local copies, waits for them, and re-layouts  15.8 us (5%)
  between operations  14.2 us (4%)
  starting transfers between devices  9.76 us (3%)
    all_to_all x1, blocking collectives, per_device(): lax.all_to_all(outgoing, ('exp', 'tk'), split_axis=0, concat_axis=0, tile...  111 us
    all_to_all x1, waiting for transfers between devices, per_device(): lax.all_to_all(computed, ('exp', 'tk'), split_axis=0, concat_axis=0, tile...  96.4 us
    all_gather x1, blocking collectives, per_device(): lax.all_gather(talker_rows, 'tk', axis=0, tiled=True)  19.9 us
    reduce_scatter x1, waiting for transfers between devices, per_device(): lax.psum_scatter(partial_rows.reshape(replicas * count, width).astype(jnp...  18.8 us
    all_gather x1, blocking collectives, per_device(): lax.all_gather(moe_in, 'rep', axis=0, tiled=True)  16.4 us
    all_to_all x1, starting transfers between devices, per_device(): lax.all_to_all(computed, ('exp', 'tk'), split_axis=0, concat_axis=0, tile...  9.54 us
    all_gather x1, blocking collectives, per_device(): lax.all_gather(route, 'rep', axis=0, tiled=True)  9.05 us
    dot_general x1, matrix products, expert_apply(): lax.dot_general(active, down, (((1,), (1,)), ((), ())), preferred_element...  7.3 us
  transfers between devices with their start and end apart: 2, of which 2 were waited for; matrix products, arithmetic and copies ran while one was open for 0% of the time, Pallas kernels for 0%

commit v1 on v0

--- a/solution.py
+++ b/solution.py
@@ -1,10 +1,39 @@
+import functools
+
 import jax
 import jax.numpy as jnp
 from jax import lax
+from jax.experimental import pallas as pl
+from jax.experimental.pallas import tpu as pltpu
 from jax.sharding import PartitionSpec as P
 
 HD = 128
 KVH = 4
+AXES = ("exp", "rep", "tk")
+NX, NZL, NZH, NY = 4, 4, 2, 8
+NZ = NZL * NZH
+
+
+def position(x, y, z, core):
+    return ((x * NZL + z % NZL) * 2 * NZH + (z // NZL) * 2 + core) * NY + y
+
+
+def line_groups():
+    along_y = [[position(x, y, z, 0) for y in range(NY)] for x in range(NX) for z in range(NZ)]
+    along_z = [[position(x, y, z, 1) for z in range(NZ)] for x in range(NX) for y in range(NY)]
+    return along_y + along_z
+
+
+def plane_groups():
+    plane_xz = [[position(x, y, z, 0) for x in range(NX) for z in range(NZ)] for y in range(NY)]
+    plane_xy = [[position(x, y, z, 1) for x in range(NX) for y in range(NY)] for z in range(NZ)]
+    return plane_xz + plane_xy
+
+
+def exchange(blocks, groups):
+    return lax.all_to_all(
+        blocks, AXES, split_axis=0, concat_axis=0, axis_index_groups=groups, tiled=True
+    )
 
 
 def normalize(values, gain):
@@ -56,24 +85,65 @@
     return jnp.sum(spread, axis=1).astype(jnp.bfloat16)
 
 
-def slot_table(route, capacity):
-    member = route > 0
-    ranking = jnp.cumsum(member.astype(jnp.int32), axis=-2) - 1
-    return jnp.logical_and(
-        member[..., None], ranking[..., None] == jnp.arange(capacity, dtype=jnp.int32)
-    )
-
-
-def expert_apply(slots, gate, raise_weight, down):
-    width = slots.shape[-1]
-    flat = slots.reshape(-1, width)
-    gated = jnp.dot(flat, gate, preferred_element_type=jnp.float32)
-    raised = jnp.dot(flat, raise_weight, preferred_element_type=jnp.float32)
-    active = (jax.nn.silu(gated) * raised).astype(jnp.bfloat16)
-    output = lax.dot_general(
-        active, down, (((1,), (1,)), ((), ())), preferred_element_type=jnp.float32
-    )
-    return output.astype(jnp.bfloat16).reshape(slots.shape)
+def slot_masks(route, slots):
+    rows, experts = route.shape
+    exp, rep, tk = (lax.axis_index(a) for a in AXES)
+    core, z_lo = rep % 2, exp % NZL
+    target = lax.broadcasted_iota(jnp.int32, (NX * NZ, experts), 0)
+    x, rest = target // NZ, target % NZ
+    holds = jnp.where(core == 0, (x * NZL + rest % NZL) * NY + tk, (x * NZL + z_lo) * NY + rest)
+    chosen = (holds == lax.broadcasted_iota(jnp.int32, holds.shape, 1)).astype(jnp.bfloat16)
+    share = lax.dot_general(
+        chosen, route, (((1,), (1,)), ((), ())), preferred_element_type=jnp.float32
+    )
+    member = share > 0
+    before = lax.broadcasted_iota(jnp.int32, (rows, rows), 0)
+    until = before <= lax.broadcasted_iota(jnp.int32, (rows, rows), 1)
+    rank = jnp.dot(
+        member.astype(jnp.bfloat16), until.astype(jnp.bfloat16), preferred_element_type=jnp.float32
+    ).astype(jnp.int32)
+    slot = lax.broadcasted_iota(jnp.int32, (target.shape[0], slots, rows), 1) + 1
+    inside = jnp.logical_and(member[:, None, :], rank[:, None, :] == slot)
+    pick = inside.astype(jnp.bfloat16).reshape(-1, rows)
+    weight = jnp.where(inside, share[:, None, :], 0.0).astype(jnp.bfloat16).reshape(-1, rows)
+    return pick, weight
+
+
+def expert_kernel(x_ref, ga_ref, gb_ref, ua_ref, ub_ref, da_ref, db_ref, o_ref):
+    x = x_ref[...]
+    across = (((1,), (1,)), ((), ()))
+
+    def hidden(gate_ref, up_ref):
+        gated = lax.dot_general(x, gate_ref[...], across, preferred_element_type=jnp.float32)
+        raised = lax.dot_general(x, up_ref[...], across, preferred_element_type=jnp.float32)
+        return (gated / (1.0 + jnp.exp(-gated)) * raised).astype(jnp.bfloat16)
+
+    near = hidden(ga_ref, ua_ref)
+    far = hidden(gb_ref, ub_ref)
+    out = jnp.dot(near, da_ref[...], preferred_element_type=jnp.float32)
+    out = out + jnp.dot(far, db_ref[...], preferred_element_type=jnp.float32)
+    o_ref[...] = out.astype(jnp.bfloat16)
+
+
+def expert_apply(rows, weights):
+    count, width = rows.shape
+    block = 128
+    whole = [pl.BlockSpec(w.shape, lambda i: (0, 0)) for w in weights]
+    units = weights[0].shape[0]
+    return pl.pallas_call(
+        expert_kernel,
+        grid=(count // block,),
+        in_specs=[pl.BlockSpec((block, width), lambda i: (i, 0))] + whole,
+        out_specs=pl.BlockSpec((block, width), lambda i: (i, 0)),
+        out_shape=jax.ShapeDtypeStruct((count, width), jnp.bfloat16),
+        compiler_params=pltpu.CompilerParams(vmem_limit_bytes=40 * 1024 * 1024),
+        cost_estimate=pl.CostEstimate(
+            flops=2 * count * width * units * 6,
+            bytes_accessed=4 * count * width + 12 * units * width,
+            transcendentals=2 * count * units,
+        ),
+        name="experts",
+    )(rows, *weights)
 
 
 def per_device(
@@ -94,54 +164,38 @@
     talker_gain,
     talker_proj,
 ):
-    count = hidden_input_rows.shape[0]
-    width = hidden_input_rows.shape[1]
+    count, width = hidden_input_rows.shape
     experts = lax.axis_size("exp") * lax.axis_size("tk")
-    replicas = lax.axis_size("rep")
-    chosen_count = expert_ids.shape[1]
-    capacity = min(count, max(2, 2 * count * chosen_count // experts))
+    lines, planes = line_groups(), plane_groups()
+
+    other_core = [(r, r ^ 1) for r in range(2 * NZH)]
+    weights = []
+    for own in (expert_gate, expert_up, expert_down):
+        own = own[0].T
+        weights += [own, lax.ppermute(own, "rep", other_core)]
+
     attended = attend(queries, new_keys, new_values, cache_keys, cache_values, cache_lengths)
     residual = hidden_input_rows.astype(jnp.float32) + attended
     moe_in = normalize(residual, moe_gain).astype(jnp.bfloat16)
     route = dense_route(expert_ids, routing_weights, experts)
-    gate_local = expert_gate[0]
-    up_local = expert_up[0]
-    down_local = expert_down[0]
-    group_input_rows, group_route = (
-        lax.all_gather(moe_in, "rep", axis=0, tiled=True),
-        lax.all_gather(route, "rep", axis=0, tiled=True),
-    )
-    group_input_rows = group_input_rows.reshape(replicas, count, width)
-    group_route = group_route.reshape(replicas, count, experts)
-    table = slot_table(group_route, capacity)
-    outgoing = jnp.einsum(
-        "rnec,rnd->ercd",
-        table.astype(jnp.bfloat16),
-        group_input_rows,
-        preferred_element_type=jnp.float32,
-    )
-    outgoing = outgoing.astype(jnp.bfloat16).reshape(experts, replicas * capacity, width)
-    computed = expert_apply(
-        lax.all_to_all(outgoing, ("exp", "tk"), split_axis=0, concat_axis=0, tiled=True),
-        gate_local,
-        up_local,
-        down_local,
-    )
-    returned = lax.all_to_all(computed, ("exp", "tk"), split_axis=0, concat_axis=0, tiled=True)
-    weighted = jnp.where(table, group_route[..., None], jnp.zeros((), jnp.bfloat16))
-    partial_rows = jnp.einsum(
-        "rnec,ercd->rnd",
-        weighted,
-        returned.reshape(experts, replicas, capacity, width),
-        preferred_element_type=jnp.float32,
-    )
-    combined = lax.psum_scatter(
-        partial_rows.reshape(replicas * count, width).astype(jnp.bfloat16),
-        "rep",
-        scatter_dimension=0,
-        tiled=True,
-    ).astype(jnp.float32)
-    layer_out = (residual + combined).astype(jnp.bfloat16)
+
+    sent = jnp.concatenate([moe_in, route], axis=1)
+    line = len(lines[0])
+    held = exchange(jnp.broadcast_to(sent[None], (line,) + sent.shape), lines)
+    held = held.reshape(line * count, width + experts)
+    slots = 2 * line
+    pick, weight = slot_masks(held[:, width:], slots)
+    outgoing = jnp.dot(pick, held[:, :width], preferred_element_type=jnp.float32)
+    outgoing = outgoing.astype(jnp.bfloat16).reshape(-1, slots, width)
+    arrived = exchange(outgoing, planes).reshape(-1, width)
+    computed = expert_apply(arrived, weights)
+    returned = exchange(computed.reshape(-1, slots, width), planes).reshape(-1, width)
+    partial_rows = lax.dot_general(
+        weight, returned, (((0,), (0,)), ((), ())), preferred_element_type=jnp.float32
+    ).astype(jnp.bfloat16)
+    pieces = exchange(partial_rows.reshape(line, count, width), lines)
+    layer_out = (residual + jnp.sum(pieces.astype(jnp.float32), axis=0)).astype(jnp.bfloat16)
+
     talker_rows = normalize(prev_hidden, talker_gain).astype(jnp.bfloat16)
     talker_in = jnp.dot(
         lax.all_gather(talker_rows, "tk", axis=0, tiled=True),

time: 333 us -> 163 us (0.49)
  the two profiles are of different devices: /device:TPU:1 before, /device:TPU:88 now
where the time goes in v1:
time: 163 us; the launch traced here: 162 us
  waiting for transfers between devices  59.7 us (37%)
  starting transfers between devices  39.6 us (24%)
  blocking collectives  30.6 us (19%)
  local copies, waits for them, and re-layouts  13.6 us (8%)
  matrix products  8.3 us (5%)
  Pallas kernels  6.27 us (4%)
  other arithmetic  2.63 us (2%)
    all_to_all x4, waiting for transfers between devices, exchange(): lax.all_to_all(blocks, AXES, split_axis=0, concat_axis=0, axis_index_grou...  59.1 us
    all_to_all x4, starting transfers between devices, exchange(): lax.all_to_all(blocks, AXES, split_axis=0, concat_axis=0, axis_index_grou...  33.2 us
    all_gather x1, blocking collectives, per_device(): lax.all_gather(talker_rows, 'tk', axis=0, tiled=True)  30.6 us
    unnamed x37, local copies, waits for them, and re-layouts  10.9 us
    ppermute x3, starting transfers between devices, per_device(): weights += [own, lax.ppermute(own, 'rep', other_core)]  6.35 us
    pallas_call x1, Pallas kernels, expert_apply(): pl.pallas_call(expert_kernel, grid=(count // block,), in_specs=[pl.BlockS...  6.27 us
  transfers between devices with their start and end apart: 7, of which 4 were waited for; matrix products, arithmetic and copies ran while one was open for 1% of the time, Pallas kernels for 0%

profile of v1, /device:TPU:88, one launch (start us, length us, event | category | flops | bytes accessed | tf_op | source)
XLA Modules:
  0.0 161.6 jit_solution(88913497513868732)
XLA Ops:
  0.7 0.8 iota_compare_fusion.3
  1.5 0.9 reshape.92
  2.4 0.7 reshape.107
  3.3 2.0 %select_reduce_fusion = (f32[16,4,4]{2,1,0:T(4,128)S(1)}, f32[16,4,4,64]{3,2,1,0:T(4,128)S(1)}) fusion(pred[16,64]{1,0:T(8,128)(4,1)S(1)} %iota_compare_fusion.3, bf16[16,4,4,128]{3,2,1,0:T(4,128)(2,1)S(1)} %reshape.92, bf16[16,64,512]{2,1,0:T(8,128)(2,1)} %param.20), kind=kOutput, calls=%fused_computation.28 | convolution fusion | flops 4243200 | bytes 1181696 | tf_op jit(solution)/shard_map/bkgd,bjkd->bkgj/dot_general | solution.py:58
  6.8 0.8 broadcast_in_dim.70
  7.6 7.3 %all-to-all-start = ((bf16[8,16,2176]{2,1,0:T(8,128)(2,1)}), bf16[8,16,2176]{2,1,0:T(8,128)(2,1)S(1)}, u32[]{:S(2)}, u32[]{:S(2)}) async-start(bf16[8,16,2176]{2,1,0:T(8,128)(2,1)} %broadcast_in_dim.70), calls=%async_computation | async-start | bytes 1114112 | tf_op jit(solution)/shard_map/all_to_all | solution.py:34
  15.1 9.8 %all-to-all-done = bf16[8,16,2176]{2,1,0:T(8,128)(2,1)S(1)} async-done(((bf16[8,16,2176]{2,1,0:T(8,128)(2,1)}), bf16[8,16,2176]{2,1,0:T(8,128)(2,1)S(1)}, u32[]{:S(2)}, u32[]{:S(2)}) %all-to-all-start) | async-done | bytes 557088 | tf_op jit(solution)/shard_map/all_to_all | solution.py:34
  25.4 2.0 %convolution_convert_fusion = bf16[512,2048]{1,0:T(8,128)(2,1)} fusion(pred[512,128]{1,0:T(32,128)(4,1)S(1)} %fusion.6, bf16[128,2176]{1,0:T(8,128)(2,1)S(1)} %bitcast.62), kind=kOutput, calls=%fused_computation | convolution fusion | flops 269484032 | bytes 2686976 | tf_op jit(solution)/shard_map/dot_general | solution.py:188
  27.4 12.6 %all-to-all-start.1 = ((bf16[32,16,2048]{2,1,0:T(8,128)(2,1)}), bf16[32,16,2048]{2,1,0:T(8,128)(2,1)S(1)}, u32[]{:S(2)}, u32[]{:S(2)}) async-start(bf16[32,16,2048]{2,1,0:T(8,128)(2,1)} %bitcast.60), calls=%async_computation.1 | async-start | bytes 4194304 | tf_op jit(solution)/shard_map/all_to_all | solution.py:34
  40.0 2.0 %collective-permute-start = (bf16[192,2048]{1,0:T(8,128)(2,1)}, bf16[192,2048]{1,0:T(8,128)(2,1)S(1)}, u32[]{:S(2)}, u32[]{:S(2)}) collective-permute-start(bf16[192,2048]{1,0:T(8,128)(2,1)} %bitcast.54), channel_id=1, source_target_pairs={{0,8},{8,0},{16,24},{24,16},{1,9},{9,1},{17,25},{25,17},{2,10},{10... | collective-permute-start | bytes 2359304 | tf_op jit(solution)/shard_map/ppermute | solution.py:175
  42.0 2.3 %collective-permute-start.1 = (bf16[192,2048]{1,0:T(8,128)(2,1)}, bf16[192,2048]{1,0:T(8,128)(2,1)S(1)}, u32[]{:S(2)}, u32[]{:S(2)}) collective-permute-start(bf16[192,2048]{1,0:T(8,128)(2,1)} %bitcast.56), channel_id=1, source_target_pairs={{0,8},{8,0},{16,24},{24,16},{1,9},{9,1},{17,25},{25,17},{2,10},{10... | collective-permute-start | bytes 2359304 | tf_op jit(solution)/shard_map/ppermute | solution.py:175
  44.4 2.0 %collective-permute-start.2 = (bf16[192,2048]{1,0:T(8,128)(2,1)}, bf16[192,2048]{1,0:T(8,128)(2,1)S(1)}, u32[]{:S(2)}, u32[]{:S(2)}) collective-permute-start(bf16[192,2048]{1,0:T(8,128)(2,1)} %bitcast.58), channel_id=1, source_target_pairs={{0,8},{8,0},{16,24},{24,16},{1,9},{9,1},{17,25},{25,17},{2,10},{10... | collective-permute-start | bytes 2359304 | tf_op jit(solution)/shard_map/ppermute | solution.py:175
  46.4 0.9 copy-done.5
  47.3 0.9 copy-done.7
  48.2 0.6 collective-permute-done.2.db_ref
  48.8 0.9 copy-done.9
  49.6 19.9 %all-to-all-done.1 = bf16[32,16,2048]{2,1,0:T(8,128)(2,1)S(1)} async-done(((bf16[32,16,2048]{2,1,0:T(8,128)(2,1)}), bf16[32,16,2048]{2,1,0:T(8,128)(2,1)S(1)}, u32[]{:S(2)}, u32[]{:S(2)}) %all-to-all-start.1) | async-done | bytes 2097184 | tf_op jit(solution)/shard_map/all_to_all | solution.py:34
  69.5 1.1 copy-done.2
  70.6 1.1 copy-done.3
  71.8 1.1 copy-done.4
  72.9 1.1 copy-done.6
  74.0 1.1 copy-done.8
  75.2 1.1 copy-done.10
  76.3 6.3 %experts.1 = bf16[512,2048]{1,0:T(8,128)(2,1)S(1)} custom-call(bf16[512,2048]{1,0:T(8,128)(2,1)S(1)} %bitcast.52, bf16[192,2048]{1,0:T(8,128)(2,1)S(1)} %bitcast.55, bf16[192,2048]{1,0:T(8,128)(2,1)S(1)} %copy-done.6, bf16[192,2048]{1,0:T(8,128)(2,1)S(1)} %bitcast.57, bf16[192,2048]{1,0:T(8,128)(2,1)S(1)} %copy-done.8, bf16[192,2048]{1,0:T(8,128)(2,1)S(1)} %bitcast.59, ...), custom_call_target="tpu_custom_call" | custom-call | flops 2415919104 | bytes 8912896 | tf_op jit(solution)/shard_map/experts/pallas_call | solution.py:133
  82.6 1.3 copy-done.1
  83.9 7.2 %all-to-all-start.2 = ((bf16[32,16,2048]{2,1,0:T(8,128)(2,1)}), bf16[32,16,2048]{2,1,0:T(8,128)(2,1)S(1)}, u32[]{:S(2)}, u32[]{:S(2)}) async-start(bf16[32,16,2048]{2,1,0:T(8,128)(2,1)} %bitcast.53), calls=%async_computation.2 | async-start | bytes 4194304 | tf_op jit(solution)/shard_map/all_to_all | solution.py:34
  91.4 29.4 %all-to-all-done.2 = bf16[32,16,2048]{2,1,0:T(8,128)(2,1)S(1)} async-done(((bf16[32,16,2048]{2,1,0:T(8,128)(2,1)}), bf16[32,16,2048]{2,1,0:T(8,128)(2,1)S(1)}, u32[]{:S(2)}, u32[]{:S(2)}) %all-to-all-start.2) | async-done | bytes 2097184 | tf_op jit(solution)/shard_map/all_to_all | solution.py:34
  120.8 1.3 fusion
  122.1 6.1 %all-to-all-start.3 = ((bf16[8,16,2048]{2,1,0:T(8,128)(2,1)}), bf16[8,16,2048]{2,1,0:T(8,128)(2,1)S(1)}, u32[]{:S(2)}, u32[]{:S(2)}) async-start(bf16[8,16,2048]{2,1,0:T(8,128)(2,1)} %bitcast.63), calls=%async_computation.3 | async-start | bytes 1048576 | tf_op jit(solution)/shard_map/all_to_all | solution.py:34
  128.3 30.6 %all_gather.3 = bf16[128,2048]{1,0:T(8,128)(2,1)S(1)} all-gather(bf16[16,2048]{1,0:T(8,128)(2,1)S(1)} %fusion.9), channel_id=1, replica_groups=mesh['exp'=16,'rep'=4,'tk'=8] {'tk'}, dimensions={0}, use_global_device_ids=true | all-gather | bytes 589824 | tf_op jit(solution)/shard_map/all_gather | solution.py:201
  158.9 1.9 %convolution_convert_fusion.1 = bf16[128,128]{1,0:T(8,128)(2,1)} fusion(bf16[128,2048]{1,0:T(8,128)(2,1)S(1)} %all_gather.3, bf16[2048,128]{1,0:T(8,128)(2,1)} %param.31), kind=kOutput, calls=%fused_computation.5 | convolution fusion | flops 67125248 | bytes 1081344 | tf_op jit(solution)/shard_map/dot_general | solution.py:200
  161.0 0.6 add_convert_fusion
  (58 shorter events, 2.5 us)
Async XLA Ops:
  0.6 5.1 %copy-start = (bf16[16,64,512]{2,1,0:T(8,128)(2,1)S(1)}, bf16[16,64,512]{2,1,0:T(8,128)(2,1)}, u32[]{:S(2)}) copy-start(bf16[16,64,512]{2,1,0:T(8,128)(2,1)} %param.21) | copy-start | bytes 3145732
  0.6 5.0 %copy-start.13 = (bf16[16,512]{1,0:T(8,128)(2,1)S(1)}, bf16[16,512]{1,0:T(8,128)(2,1)}, u32[]{:S(2)}) copy-start(bf16[16,512]{1,0:T(8,128)(2,1)} %param.19) | copy-start | bytes 49156
  5.3 1.0 copy-start.11
  5.3 1.1 copy-start.14
  5.3 1.1 copy-start.15
  5.3 1.2 copy-start.17
  7.6 17.2 %all-to-all-start = ((bf16[8,16,2176]{2,1,0:T(8,128)(2,1)}), bf16[8,16,2176]{2,1,0:T(8,128)(2,1)S(1)}, u32[]{:S(2)}, u32[]{:S(2)}) async-start(bf16[8,16,2176]{2,1,0:T(8,128)(2,1)} %broadcast_in_dim.70), calls=%async_computation | async-start | bytes 1114112 | tf_op jit(solution)/shard_map/all_to_all | solution.py:34
  27.4 42.1 %all-to-all-start.1 = ((bf16[32,16,2048]{2,1,0:T(8,128)(2,1)}), bf16[32,16,2048]{2,1,0:T(8,128)(2,1)S(1)}, u32[]{:S(2)}, u32[]{:S(2)}) async-start(bf16[32,16,2048]{2,1,0:T(8,128)(2,1)} %bitcast.60), calls=%async_computation.1 | async-start | bytes 4194304 | tf_op jit(solution)/shard_map/all_to_all | solution.py:34
  40.0 6.4 %collective-permute-start = (bf16[192,2048]{1,0:T(8,128)(2,1)}, bf16[192,2048]{1,0:T(8,128)(2,1)S(1)}, u32[]{:S(2)}, u32[]{:S(2)}) collective-permute-start(bf16[192,2048]{1,0:T(8,128)(2,1)} %bitcast.54), channel_id=1, source_target_pairs={{0,8},{8,0},{16,24},{24,16},{1,9},{9,1},{17,25},{25,17},{2,10},{10... | collective-permute-start | bytes 2359304 | tf_op jit(solution)/shard_map/ppermute | solution.py:175
  42.0 5.2 %collective-permute-start.1 = (bf16[192,2048]{1,0:T(8,128)(2,1)}, bf16[192,2048]{1,0:T(8,128)(2,1)S(1)}, u32[]{:S(2)}, u32[]{:S(2)}) collective-permute-start(bf16[192,2048]{1,0:T(8,128)(2,1)} %bitcast.56), channel_id=1, source_target_pairs={{0,8},{8,0},{16,24},{24,16},{1,9},{9,1},{17,25},{25,17},{2,10},{10... | collective-permute-start | bytes 2359304 | tf_op jit(solution)/shard_map/ppermute | solution.py:175
  44.4 4.4 %collective-permute-start.2 = (bf16[192,2048]{1,0:T(8,128)(2,1)}, bf16[192,2048]{1,0:T(8,128)(2,1)S(1)}, u32[]{:S(2)}, u32[]{:S(2)}) collective-permute-start(bf16[192,2048]{1,0:T(8,128)(2,1)} %bitcast.58), channel_id=1, source_target_pairs={{0,8},{8,0},{16,24},{24,16},{1,9},{9,1},{17,25},{25,17},{2,10},{10... | collective-permute-start | bytes 2359304 | tf_op jit(solution)/shard_map/ppermute | solution.py:175
  46.4 0.9 copy-start.5
  47.3 0.9 copy-start.7
  48.8 0.9 copy-start.9
  69.5 1.1 copy-start.2
  70.6 1.1 copy-start.3
  71.8 1.1 copy-start.4
  72.9 1.1 copy-start.6
  74.0 1.1 copy-start.8
  75.2 1.1 copy-start.10
  82.6 1.3 copy-start.1
  83.9 7.3 %copy-start.16 = (bf16[2048]{0:T(1024)(128)(2,1)S(1)}, bf16[2048]{0:T(1024)(128)(2,1)}, u32[]{:S(2)}) copy-start(bf16[2048]{0:T(1024)(128)(2,1)} %param.30) | copy-start | bytes 12292
  83.9 7.3 %copy-start.12 = (bf16[16,2048]{1,0:T(8,128)(2,1)S(1)}, bf16[16,2048]{1,0:T(8,128)(2,1)}, u32[]{:S(2)}) copy-start(bf16[16,2048]{1,0:T(8,128)(2,1)} %param.29) | copy-start | bytes 196612
  83.9 36.8 %all-to-all-start.2 = ((bf16[32,16,2048]{2,1,0:T(8,128)(2,1)}), bf16[32,16,2048]{2,1,0:T(8,128)(2,1)S(1)}, u32[]{:S(2)}, u32[]{:S(2)}) async-start(bf16[32,16,2048]{2,1,0:T(8,128)(2,1)} %bitcast.53), calls=%async_computation.2 | async-start | bytes 4194304 | tf_op jit(solution)/shard_map/all_to_all | solution.py:34
  122.1 38.8 %all-to-all-start.3 = ((bf16[8,16,2048]{2,1,0:T(8,128)(2,1)}), bf16[8,16,2048]{2,1,0:T(8,128)(2,1)S(1)}, u32[]{:S(2)}, u32[]{:S(2)}) async-start(bf16[8,16,2048]{2,1,0:T(8,128)(2,1)} %bitcast.63), calls=%async_computation.3 | async-start | bytes 1048576 | tf_op jit(solution)/shard_map/all_to_all | solution.py:34

commit v2 on v1

v2 whole, which is shorter than its diff:
```python
import functools

import jax
import jax.numpy as jnp
from jax import lax
from jax.experimental import pallas as pl
from jax.experimental.pallas import tpu as pltpu
from jax.sharding import PartitionSpec as P

HD = 128
KVH = 4
BIG_VMEM = 60 * 1024 * 1024
SMALL_VMEM = 24 * 1024 * 1024
AXES = ("exp", "rep", "tk")
NX, NZL, NZH, NY = 4, 4, 2, 8
NZ = NZL * NZH


def position(x, y, z, core):
    return ((x * NZL + z % NZL) * 2 * NZH + (z // NZL) * 2 + core) * NY + y


def line_groups():
    along_y = [[position(x, y, z, 0) for y in range(NY)] for x in range(NX) for z in range(NZ)]
    along_z = [[position(x, y, z, 1) for z in range(NZ)] for x in range(NX) for y in range(NY)]
    return along_y + along_z


def plane_groups():
    plane_xz = [[position(x, y, z, 0) for x in range(NX) for z in range(NZ)] for y in range(NY)]
    plane_xy = [[position(x, y, z, 1) for x in range(NX) for y in range(NY)] for z in range(NZ)]
    return plane_xz + plane_xy


def exchange(blocks, groups):
    return lax.all_to_all(
        blocks, AXES, split_axis=0, concat_axis=0, axis_index_groups=groups, tiled=True
    )


def attend_kernel(
    lengths_ref,
    hidden_ref,
    q_ref,
    new_key_ref,
    new_value_ref,
    keys_ref,
    values_ref,
    gain_ref,
    ids_ref,
    routing_ref,
    sent_ref,
    residual_ref,
):
    count, span, _ = keys_ref.shape
    width = hidden_ref.shape[1]
    group = width // HD // KVH
    scale = HD ** (-0.5)
    row = lax.broadcasted_iota(jnp.int32, (count, count * span), 0)
    offset = lax.broadcasted_iota(jnp.int32, (count, count * span), 1) - row * span
    first = lax.broadcasted_iota(jnp.int32, (count, 1), 0)
    lengths = jnp.zeros((count, 1), jnp.int32)
    for r in range(count):
        lengths = jnp.where(first == r, lengths_ref[r], lengths)
    valid = jnp.logical_and(offset >= 0, offset < lengths)
    bias = jnp.concatenate([jnp.where(valid, 0.0, -1e30)] * group, axis=0)
    square = jnp.zeros((count, HD), jnp.float32)
    for head in range(KVH):
        lanes = [slice((head * group + h) * HD, (head * group + h + 1) * HD) for h in range(group)]
        query = jnp.concatenate([q_ref[:, lane] for lane in lanes], axis=0)
        own_lane = slice(head * HD, (head + 1) * HD)
        keys = keys_ref[:, :, own_lane].reshape(count * span, HD)
        values = values_ref[:, :, own_lane].reshape(count * span, HD)
        cached = lax.dot_general(
            query, keys, (((1,), (1,)), ((), ())), preferred_element_type=jnp.float32
        )
        cached = cached * scale + bias
        new_key = jnp.concatenate([new_key_ref[:, own_lane]] * group, axis=0).astype(jnp.float32)
        own = jnp.sum(query.astype(jnp.float32) * new_key, axis=-1, keepdims=True) * scale
        top = jnp.maximum(jnp.max(cached, axis=-1, keepdims=True), own)
        weight = jnp.exp(cached - top)
        own_weight = jnp.exp(own - top)
        share = 1.0 / (jnp.sum(weight, axis=-1, keepdims=True) + own_weight)
        probs = (weight * share).astype(jnp.bfloat16)
        own_prob = (own_weight * share).astype(jnp.bfloat16).astype(jnp.float32)
        mixed = jnp.dot(probs, values, preferred_element_type=jnp.float32)
        new_value = jnp.concatenate([new_value_ref[:, own_lane]] * group, axis=0)
        mixed = mixed + own_prob * new_value.astype(jnp.float32)
        for h, lane in enumerate(lanes):
            after = hidden_ref[:, lane].astype(jnp.float32) + mixed[h * count : (h + 1) * count]
            residual_ref[:, lane] = after
            square = square + after * after
    norm = lax.rsqrt(jnp.sum(square, axis=-1, keepdims=True) / width + 1e-06)
    gain = gain_ref[...].astype(jnp.float32).reshape(1, width)
    moe_in = (residual_ref[...] * norm * gain).astype(jnp.bfloat16)
    ids, routing = ids_ref[...], routing_ref[...].astype(jnp.float32)
    experts = sent_ref.shape[2] - width
    expert = lax.broadcasted_iota(jnp.int32, (experts, count), 0)
    route = jnp.zeros((experts, count), jnp.float32)
    for k in range(ids.shape[0]):
        route = route + jnp.where(expert == ids[k : k + 1], routing[k : k + 1], 0.0)
    route = route.T.astype(jnp.bfloat16)
    for copy in range(sent_ref.shape[0]):
        sent_ref[copy, :, :width] = moe_in
        sent_ref[copy, :, width:] = route


def origin(ndim, step):
    return (0,) * ndim


def attend(
    copies,
    experts,
    hidden,
    queries,
    new_keys,
    new_values,
    cache_keys,
    cache_values,
    lengths,
    gain,
    ids,
    routing,
):
    count, width = hidden.shape
    operands = (
        hidden,
        queries,
        new_keys,
        new_values,
        cache_keys,
        cache_values,
        gain,
        ids.T,
        routing.T,
    )
    return pl.pallas_call(
        attend_kernel,
        grid=(1,),
        in_specs=[pl.BlockSpec(memory_space=pltpu.SMEM)]
        + [pl.BlockSpec(o.shape, functools.partial(origin, o.ndim)) for o in operands],
        out_specs=[
            pl.BlockSpec((copies, count, width + experts), functools.partial(origin, 3)),
            pl.BlockSpec((count, width), functools.partial(origin, 2)),
        ],
        out_shape=[
            pltpu.HBM((copies, count, width + experts), jnp.bfloat16),
            jax.ShapeDtypeStruct((count, width), jnp.float32),
        ],
        compiler_params=pltpu.CompilerParams(vmem_limit_bytes=BIG_VMEM),
        name="attend",
    )(lengths, *operands)


def slot_masks(route, slots):
    rows, experts = route.shape
    exp, rep, tk = (lax.axis_index(a) for a in AXES)
    core, z_lo = rep % 2, exp % NZL
    target = lax.broadcasted_iota(jnp.int32, (NX * NZ, experts), 0)
    x, rest = target // NZ, target % NZ
    holds = jnp.where(core == 0, (x * NZL + rest % NZL) * NY + tk, (x * NZL + z_lo) * NY + rest)
    chosen = (holds == lax.broadcasted_iota(jnp.int32, holds.shape, 1)).astype(jnp.bfloat16)
    share = lax.dot_general(
        chosen, route, (((1,), (1,)), ((), ())), preferred_element_type=jnp.float32
    )
    member = share > 0
    before = lax.broadcasted_iota(jnp.int32, (rows, rows), 0)
    until = before <= lax.broadcasted_iota(jnp.int32, (rows, rows), 1)
    rank = jnp.dot(
        member.astype(jnp.bfloat16), until.astype(jnp.bfloat16), preferred_element_type=jnp.float32
    ).astype(jnp.int32)
    slot = lax.broadcasted_iota(jnp.int32, (target.shape[0], slots, rows), 1) + 1
    inside = jnp.logical_and(member[:, None, :], rank[:, None, :] == slot)
    pick = inside.astype(jnp.bfloat16).reshape(-1, rows)
    weight = jnp.where(inside, share[:, None, :], 0.0).astype(jnp.bfloat16).reshape(-1, rows)
    return pick, weight


def weight_pieces(units, block):
    pieces = []
    for first in range(0, 2 * units, block):
        for kind in range(2):
            unit = first
            while unit < first + block:
                side, row = divmod(unit, units)
                rows = min(first + block - unit, units - row)
                place = 2 * first + kind * block + unit - first
                pieces.append((2 * kind + side, row, rows, place))
                unit += rows
    return pieces


def expert_kernel(x_ref, *refs):
    weights, (o_ref, in_ref, down_ref, active_ref, out_ref, sems, out_sems) = refs[:6], refs[6:]
    units = weights[0].shape[0]
    block = 128
    pieces = weight_pieces(units, block)
    copies = [
        pltpu.make_async_copy(
            weights[array].at[pl.ds(row, rows)], in_ref.at[pl.ds(place, rows)], sems.at[i]
        )
        for i, (array, row, rows, place) in enumerate(pieces)
    ]
    down_copies = [
        pltpu.make_async_copy(
            weights[4 + i], down_ref.at[pl.ds(i * units, units)], sems.at[len(pieces) + i]
        )
        for i in range(2)
    ]
    for copy in copies + down_copies:
        copy.start()
    for first in range(0, 2 * units, block):
        for copy, piece in zip(copies, pieces):
            if 2 * first <= piece[3] < 2 * (first + block):
                copy.wait()
        both = lax.dot_general(
            x_ref[...],
            in_ref[2 * first : 2 * (first + block)],
            (((1,), (1,)), ((), ())),
            preferred_element_type=jnp.float32,
        )
        gated, raised = both[:, :block], both[:, block:]
        active_ref[:, first : first + block] = (
            gated / (1.0 + jnp.exp(-gated)) * raised
        ).astype(jnp.bfloat16)
    for copy in down_copies:
        copy.wait()
    parts, _, part = out_ref.shape
    out_copies = []
    for i in range(parts):
        lanes = pl.ds(i * part, part)
        out = jnp.dot(active_ref[...], down_ref[:, lanes], preferred_element_type=jnp.float32)
        out_ref[i] = out.astype(jnp.bfloat16)
        out_copies.append(pltpu.make_async_copy(out_ref.at[i], o_ref.at[:, lanes], out_sems.at[i]))
        out_copies[-1].start()
    for copy in out_copies:
        copy.wait()


def expert_apply(rows, weights):
    count, width = rows.shape
    units = weights[0].shape[0]
    parts = 4
    return pl.pallas_call(
        expert_kernel,
        in_specs=[pl.BlockSpec(memory_space=pltpu.VMEM)]
        + [pl.BlockSpec(memory_space=pltpu.HBM)] * 6,
        out_specs=pl.BlockSpec(memory_space=pltpu.HBM),
        out_shape=pltpu.HBM((count, width), jnp.bfloat16),
        scratch_shapes=[
            pltpu.VMEM((4 * units, width), jnp.bfloat16),
            pltpu.VMEM((2 * units, width), jnp.bfloat16),
            pltpu.VMEM((count, 2 * units), jnp.bfloat16),
            pltpu.VMEM((parts, count, width // parts), jnp.bfloat16),
            pltpu.SemaphoreType.DMA((16,)),
            pltpu.SemaphoreType.DMA((parts,)),
        ],
        compiler_params=pltpu.CompilerParams(vmem_limit_bytes=SMALL_VMEM),
        cost_estimate=pl.CostEstimate(
            flops=12 * count * width * units,
            bytes_accessed=4 * count * width + 12 * units * width,
            transcendentals=2 * count * units,
        ),
        name="experts",
    )(rows, *weights)


def per_device(
    hidden_input_rows,
    queries,
    new_keys,
    new_values,
    cache_keys,
    cache_values,
    cache_lengths,
    moe_gain,
    expert_ids,
    routing_weights,
    expert_gate,
    expert_up,
    expert_down,
    prev_hidden,
    talker_gain,
    talker_proj,
):
    count, width = hidden_input_rows.shape
    experts = lax.axis_size("exp") * lax.axis_size("tk")
    lines, planes = line_groups(), plane_groups()
    line = len(lines[0])

    sent, residual = attend(
        line,
        experts,
        hidden_input_rows,
        queries,
        new_keys,
        new_values,
        cache_keys,
        cache_values,
        cache_lengths,
        moe_gain,
        expert_ids,
        routing_weights,
    )

    wide = prev_hidden.astype(jnp.float32)
    unit = wide * lax.rsqrt(jnp.mean(wide * wide, axis=-1, keepdims=True) + 1e-06)
    talker_units = lax.all_gather(unit, "tk", axis=0, tiled=True)

    own = [w[0].T for w in (expert_gate, expert_up, expert_down)]
    sent, own = lax.optimization_barrier((sent, own))
    other = [lax.ppermute(w, "rep", [(r, r ^ 1) for r in range(2 * NZH)]) for w in own]
    held = exchange(sent, lines).reshape(line * count, width + experts)
    held, own, other = lax.optimization_barrier((held, own, other))
    slots = 2 * line
    pick, weight = slot_masks(held[:, width:], slots)
    outgoing = jnp.dot(pick, held[:, :width], preferred_element_type=jnp.float32)
    outgoing = outgoing.astype(jnp.bfloat16).reshape(-1, slots, width)
    arrived = exchange(outgoing, planes).reshape(-1, width)
    weights = [own[0], other[0], own[1], other[1], own[2], other[2]]
    computed = expert_apply(arrived, weights)
    returned = exchange(computed.reshape(-1, slots, width), planes).reshape(-1, width)
    partial_rows = lax.dot_general(
        weight, returned, (((0,), (0,)), ((), ())), preferred_element_type=jnp.float32
    ).astype(jnp.bfloat16)
    pieces = exchange(partial_rows.reshape(line, count, width), lines)
    layer_out = (residual + jnp.sum(pieces.astype(jnp.float32), axis=0)).astype(jnp.bfloat16)

    talker_rows = (talker_units * talker_gain.astype(jnp.float32)).astype(jnp.bfloat16)
    talker_in = jnp.dot(talker_rows, talker_proj, preferred_element_type=jnp.float32)
    return (layer_out, talker_in.astype(jnp.bfloat16))


def solution(mesh):
    placed = (
        P(("exp", "rep", "tk"), None),
        P(("exp", "rep", "tk"), None),
        P(("exp", "rep", "tk"), None),
        P(("exp", "rep", "tk"), None),
        P(("exp", "rep", "tk"), None, None),
        P(("exp", "rep", "tk"), None, None),
        P(("exp", "rep", "tk")),
        P(),
        P(("exp", "rep", "tk"), None),
        P(("exp", "rep", "tk"), None),
        P(("exp", "tk"), None, "rep"),
        P(("exp", "tk"), None, "rep"),
        P(("exp", "tk"), None, "rep"),
        P(("exp", "rep", "tk"), None),
        P(),
        P(None, "tk"),
    )
    return jax.shard_map(
        per_device,
        mesh=mesh,
        in_specs=placed,
        out_specs=(P(("exp", "rep", "tk"), None), P(("exp", "rep"), "tk")),
        check_vma=False,
    )
```

time: 163 us -> 144 us (0.88)
  the two profiles are of different devices: /device:TPU:88 before, /device:TPU:1 now
where the time goes in v2:
time: 144 us; the launch traced here: 143 us
  waiting for transfers between devices  46 us (32%)
  blocking collectives  36.8 us (26%)
  starting transfers between devices  27.9 us (19%)
  between operations  14.3 us (10%)
  Pallas kernels  11.4 us (8%)
  matrix products  4.53 us (3%)
  other arithmetic  1.77 us (1%)
    all_to_all x3, waiting for transfers between devices, exchange(): lax.all_to_all(blocks, AXES, split_axis=0, concat_axis=0, axis_index_grou...  36.8 us
    all_to_all x1, blocking collectives, exchange(): lax.all_to_all(blocks, AXES, split_axis=0, concat_axis=0, axis_index_grou...  36.8 us
    all_to_all x3, starting transfers between devices, exchange(): lax.all_to_all(blocks, AXES, split_axis=0, concat_axis=0, axis_index_grou...  21.6 us
    all_gather x1, waiting for transfers between devices, per_device(): talker_units = lax.all_gather(unit, 'tk', axis=0, tiled=True)  6.9 us
    pallas_call x1, Pallas kernels, expert_apply(): pl.pallas_call(expert_kernel, in_specs=[pl.BlockSpec(memory_space=pltpu.V...  6.81 us
    ppermute x3, starting transfers between devices, per_device(): lax.ppermute(w, 'rep', [(r, r ^ 1) for r in range(2 * NZH)])  6.25 us
    pallas_call x1, Pallas kernels, attend(): pl.pallas_call(attend_kernel, grid=(1,), in_specs=[pl.BlockSpec(memory_sp...  4.57 us
  transfers between devices with their start and end apart: 7, of which 5 were waited for; matrix products, arithmetic and copies ran while one was open for 3% of the time, Pallas kernels for 0%

profile of v2, /device:TPU:1, one launch (start us, length us, event | category | flops | bytes accessed | tf_op | source)
XLA Modules:
  0.0 142.7 jit_solution(16758356116357601008)
XLA Ops:
  7.2 0.0 copy-start
  7.2 4.6 %attend.1 = (bf16[8,16,2176]{2,1,0:T(8,128)(2,1)}, f32[16,2048]{1,0:T(8,128)}) custom-call(s32[16]{0:T(128)} %lengths_ref.1, bf16[16,2048]{1,0:T(8,128)(2,1)} %hidden_ref.1, bf16[16,2048]{1,0:T(8,128)(2,1)} %q_ref.1, bf16[16,512]{1,0:T(8,128)(2,1)} %new_key_ref.1, bf16[16,512]{1,0:T(8,128)(2,1)} %new_value_ref.1, bf16[16,64,512]{2,1,0:T(8,128)(2,1)} %keys_ref.1, ...), custom_call_target="tpu_custom_call" | custom-call | tf_op jit(solution)/shard_map/attend/pallas_call | solution.py:138
  11.8 10.9 %all-to-all-start = ((bf16[8,16,2176]{2,1,0:T(8,128)(2,1)}), bf16[8,16,2176]{2,1,0:T(8,128)(2,1)S(1)}, u32[]{:S(2)}, u32[]{:S(2)}) async-start(bf16[8,16,2176]{2,1,0:T(8,128)(2,1)} %get-tuple-element.17), calls=%async_computation | async-start | bytes 1114112 | tf_op jit(solution)/shard_map/all_to_all | solution.py:36
  22.7 1.9 %collective-permute-start = (bf16[192,2048]{1,0:T(8,128)(2,1)S(1)}, bf16[192,2048]{1,0:T(8,128)(2,1)}, u32[]{:S(2)}, u32[]{:S(2)}) collective-permute-start(bf16[192,2048]{1,0:T(8,128)(2,1)S(1)} %bitcast.33), channel_id=1, source_target_pairs={{0,8},{8,0},{16,24},{24,16},{1,9},{9,1},{17,25},{25,17},{2,10},{10... | collective-permute-start | bytes 2359304 | tf_op jit(solution)/shard_map/ppermute | solution.py:313
  24.6 2.4 %collective-permute-start.1 = (bf16[192,2048]{1,0:T(8,128)(2,1)S(1)}, bf16[192,2048]{1,0:T(8,128)(2,1)}, u32[]{:S(2)}, u32[]{:S(2)}) collective-permute-start(bf16[192,2048]{1,0:T(8,128)(2,1)S(1)} %bitcast.35), channel_id=1, source_target_pairs={{0,8},{8,0},{16,24},{24,16},{1,9},{9,1},{17,25},{25,17},{2,10},{10... | collective-permute-start | bytes 2359304 | tf_op jit(solution)/shard_map/ppermute | solution.py:313
  27.0 1.9 %collective-permute-start.2 = (bf16[192,2048]{1,0:T(8,128)(2,1)S(1)}, bf16[192,2048]{1,0:T(8,128)(2,1)}, u32[]{:S(2)}, u32[]{:S(2)}) collective-permute-start(bf16[192,2048]{1,0:T(8,128)(2,1)S(1)} %bitcast.37), channel_id=1, source_target_pairs={{0,8},{8,0},{16,24},{24,16},{1,9},{9,1},{17,25},{25,17},{2,10},{10... | collective-permute-start | bytes 2359304 | tf_op jit(solution)/shard_map/ppermute | solution.py:313
  29.0 0.1 iota.74
  29.1 0.0 collective-permute-done.refs_1_
  29.1 0.0 collective-permute-done.1.refs_3_
  29.1 2.2 %collective-permute-done.2.refs_5_ = bf16[192,2048]{1,0:T(8,128)(2,1)} collective-permute-done((bf16[192,2048]{1,0:T(8,128)(2,1)S(1)}, bf16[192,2048]{1,0:T(8,128)(2,1)}, u32[]{:S(2)}, u32[]{:S(2)}) %collective-permute-start.2) | collective-permute-done | bytes 786464 | tf_op jit(solution)/shard_map/ppermute | solution.py:313
  31.3 4.0 %all-to-all-done = bf16[8,16,2176]{2,1,0:T(8,128)(2,1)S(1)} async-done(((bf16[8,16,2176]{2,1,0:T(8,128)(2,1)}), bf16[8,16,2176]{2,1,0:T(8,128)(2,1)S(1)}, u32[]{:S(2)}, u32[]{:S(2)}) %all-to-all-start) | async-done | bytes 557088 | tf_op jit(solution)/shard_map/all_to_all | solution.py:36
  35.4 0.2 broadcast_compare_fusion
  35.6 0.1 convolution_convert_fusion.2
  35.7 0.1 fusion.3
  35.9 0.7 convolution_convert_fusion
  36.6 36.8 %all_to_all.20 = bf16[32,16,2048]{2,1,0:T(8,128)(2,1)S(1)} all-to-all(bf16[32,16,2048]{2,1,0:T(8,128)(2,1)S(1)} %bitcast.39), channel_id=1, replica_groups={{0,32,64,96,16,48,80,112,128,160,192,224,144,176,208,240,256,288,320,35..., dimensions={0} | all-to-all | bytes 4194304 | tf_op jit(solution)/shard_map/all_to_all | solution.py:36
  73.3 6.8 %experts.1 = bf16[512,2048]{1,0:T(8,128)(2,1)} custom-call(bf16[512,2048]{1,0:T(8,128)(2,1)S(1)} %bitcast.32, bf16[192,2048]{1,0:T(8,128)(2,1)S(1)} %bitcast.34, bf16[192,2048]{1,0:T(8,128)(2,1)} %collective-permute-done.refs_1_, bf16[192,2048]{1,0:T(8,128)(2,1)S(1)} %bitcast.36, bf16[192,2048]{1,0:T(8,128)(2,1)} %collective-permute-done.1.refs_3_, ...), custom_call_target="tpu_custom_call" | custom-call | flops 2415919104 | bytes 8912896 | tf_op jit(solution)/shard_map/experts/pallas_call | solution.py:245
  80.2 0.0 copy-start.4
  80.2 7.1 %all-to-all-start.2 = ((bf16[32,16,2048]{2,1,0:T(8,128)(2,1)}), bf16[32,16,2048]{2,1,0:T(8,128)(2,1)S(1)}, u32[]{:S(2)}, u32[]{:S(2)}) async-start(bf16[32,16,2048]{2,1,0:T(8,128)(2,1)} %bitcast.42), calls=%async_computation.2 | async-start | bytes 4194304 | tf_op jit(solution)/shard_map/all_to_all | solution.py:36
  87.3 0.0 copy-start.6
  87.3 0.0 all-gather.2.cloned.1.call-start
  87.4 0.1 fusion.4
  87.5 0.8 convert_multiply_fusion
  88.3 0.0 all-gather.2.cloned.1.call-update
  88.3 29.8 %all-to-all-done.2 = bf16[32,16,2048]{2,1,0:T(8,128)(2,1)S(1)} async-done(((bf16[32,16,2048]{2,1,0:T(8,128)(2,1)}), bf16[32,16,2048]{2,1,0:T(8,128)(2,1)S(1)}, u32[]{:S(2)}, u32[]{:S(2)}) %all-to-all-start.2) | async-done | bytes 2097184 | tf_op jit(solution)/shard_map/all_to_all | solution.py:36
  118.1 1.4 fusion
  119.4 3.6 %all-to-all-start.3 = ((bf16[8,16,2048]{2,1,0:T(8,128)(2,1)}), bf16[8,16,2048]{2,1,0:T(8,128)(2,1)S(1)}, u32[]{:S(2)}, u32[]{:S(2)}) async-start(bf16[8,16,2048]{2,1,0:T(8,128)(2,1)} %bitcast.15), calls=%async_computation.3 | async-start | bytes 1048576 | tf_op jit(solution)/shard_map/all_to_all | solution.py:36
  123.1 6.9 %all-gather.2.cloned.1.call-done = f32[128,2048]{1,0:T(8,128)} async-done(((f32[16,2048]{1,0:T(8,128)}), f32[128,2048]{1,0:T(8,128)}) %all-gather.2.cloned.1.call-update) | async-done | bytes 1048592 | tf_op jit(solution)/shard_map/all_gather | solution.py:309
  130.0 2.1 %convolution_convert_fusion.1 = bf16[128,128]{1,0:T(8,128)(2,1)} fusion(bf16[2048,128]{1,0:T(8,128)(2,1)S(1)} %copy-done, f32[128,2048]{1,0:T(8,128)} %all-gather.2.cloned.1.call-done, f32[2048]{0:T(1024)S(1)} %convert_element_type.41), kind=kOutput, calls=%fused_computation.3 | convolution fusion | flops 67649536 | bytes 1613824 | tf_op jit(solution)/shard_map/dot_general | solution.py:331
  132.1 3.0 %all-to-all-done.3 = bf16[8,16,2048]{2,1,0:T(8,128)(2,1)S(1)} async-done(((bf16[8,16,2048]{2,1,0:T(8,128)(2,1)}), bf16[8,16,2048]{2,1,0:T(8,128)(2,1)S(1)}, u32[]{:S(2)}, u32[]{:S(2)}) %all-to-all-start.3) | async-done | bytes 524320 | tf_op jit(solution)/shard_map/all_to_all | solution.py:36
  135.1 0.1 convert_reduce_fusion
  135.2 0.6 add_convert_fusion
  (18 shorter events, 0.1 us)
Async XLA Ops:
  7.2 122.8 %copy-start = (bf16[2048,128]{1,0:T(8,128)(2,1)S(1)}, bf16[2048,128]{1,0:T(8,128)(2,1)}, u32[]{:S(2)}) copy-start(bf16[2048,128]{1,0:T(8,128)(2,1)} %param.31) | copy-start | bytes 1572868
  7.2 15.5 %copy-start.1 = (bf16[1,2048,192]{1,2,0:T(8,128)(2,1)S(1)}, bf16[1,2048,192]{1,2,0:T(8,128)(2,1)}, u32[]{:S(2)}) copy-start(bf16[1,2048,192]{1,2,0:T(8,128)(2,1)} %param.26) | copy-start | bytes 2359300
  7.2 17.4 %copy-start.2 = (bf16[1,2048,192]{1,2,0:T(8,128)(2,1)S(1)}, bf16[1,2048,192]{1,2,0:T(8,128)(2,1)}, u32[]{:S(2)}) copy-start(bf16[1,2048,192]{1,2,0:T(8,128)(2,1)} %param.27) | copy-start | bytes 2359300
  7.2 19.8 %copy-start.3 = (bf16[1,2048,192]{1,2,0:T(8,128)(2,1)S(1)}, bf16[1,2048,192]{1,2,0:T(8,128)(2,1)}, u32[]{:S(2)}) copy-start(bf16[1,2048,192]{1,2,0:T(8,128)(2,1)} %param.28) | copy-start | bytes 2359300
  11.8 23.6 %all-to-all-start = ((bf16[8,16,2176]{2,1,0:T(8,128)(2,1)}), bf16[8,16,2176]{2,1,0:T(8,128)(2,1)S(1)}, u32[]{:S(2)}, u32[]{:S(2)}) async-start(bf16[8,16,2176]{2,1,0:T(8,128)(2,1)} %get-tuple-element.17), calls=%async_computation | async-start | bytes 1114112 | tf_op jit(solution)/shard_map/all_to_all | solution.py:36
  22.7 6.4 %collective-permute-start = (bf16[192,2048]{1,0:T(8,128)(2,1)S(1)}, bf16[192,2048]{1,0:T(8,128)(2,1)}, u32[]{:S(2)}, u32[]{:S(2)}) collective-permute-start(bf16[192,2048]{1,0:T(8,128)(2,1)S(1)} %bitcast.33), channel_id=1, source_target_pairs={{0,8},{8,0},{16,24},{24,16},{1,9},{9,1},{17,25},{25,17},{2,10},{10... | collective-permute-start | bytes 2359304 | tf_op jit(solution)/shard_map/ppermute | solution.py:313
  24.6 4.5 %collective-permute-start.1 = (bf16[192,2048]{1,0:T(8,128)(2,1)S(1)}, bf16[192,2048]{1,0:T(8,128)(2,1)}, u32[]{:S(2)}, u32[]{:S(2)}) collective-permute-start(bf16[192,2048]{1,0:T(8,128)(2,1)S(1)} %bitcast.35), channel_id=1, source_target_pairs={{0,8},{8,0},{16,24},{24,16},{1,9},{9,1},{17,25},{25,17},{2,10},{10... | collective-permute-start | bytes 2359304 | tf_op jit(solution)/shard_map/ppermute | solution.py:313
  27.0 4.3 %collective-permute-start.2 = (bf16[192,2048]{1,0:T(8,128)(2,1)S(1)}, bf16[192,2048]{1,0:T(8,128)(2,1)}, u32[]{:S(2)}, u32[]{:S(2)}) collective-permute-start(bf16[192,2048]{1,0:T(8,128)(2,1)S(1)} %bitcast.37), channel_id=1, source_target_pairs={{0,8},{8,0},{16,24},{24,16},{1,9},{9,1},{17,25},{25,17},{2,10},{10... | collective-permute-start | bytes 2359304 | tf_op jit(solution)/shard_map/ppermute | solution.py:313
  80.2 7.2 %copy-start.4 = (bf16[16,2048]{1,0:T(8,128)(2,1)S(1)}, bf16[16,2048]{1,0:T(8,128)(2,1)}, u32[]{:S(2)}) copy-start(bf16[16,2048]{1,0:T(8,128)(2,1)} %param.29) | copy-start | bytes 196612
  80.2 37.9 %all-to-all-start.2 = ((bf16[32,16,2048]{2,1,0:T(8,128)(2,1)}), bf16[32,16,2048]{2,1,0:T(8,128)(2,1)S(1)}, u32[]{:S(2)}, u32[]{:S(2)}) async-start(bf16[32,16,2048]{2,1,0:T(8,128)(2,1)} %bitcast.42), calls=%async_computation.2 | async-start | bytes 4194304 | tf_op jit(solution)/shard_map/all_to_all | solution.py:36
  87.3 35.8 %copy-start.6 = (bf16[2048]{0:T(1024)(128)(2,1)S(1)}, bf16[2048]{0:T(1024)(128)(2,1)}, u32[]{:S(2)}) copy-start(bf16[2048]{0:T(1024)(128)(2,1)} %param.30) | copy-start | bytes 12292
  87.3 42.7 %all-gather.2.cloned.1.call-start = ((), (), s32[]{:S(2)}) async-start(), calls=%async_computation.4 | async-start | bytes 1179648 | tf_op jit(solution)/shard_map/all_gather | solution.py:309
  119.4 15.8 %copy-start.5 = (f32[16,2048]{1,0:T(8,128)S(1)}, f32[16,2048]{1,0:T(8,128)}, u32[]{:S(2)}) copy-start(f32[16,2048]{1,0:T(8,128)} %get-tuple-element.15) | copy-start | bytes 393220
  119.4 15.7 %all-to-all-start.3 = ((bf16[8,16,2048]{2,1,0:T(8,128)(2,1)}), bf16[8,16,2048]{2,1,0:T(8,128)(2,1)S(1)}, u32[]{:S(2)}, u32[]{:S(2)}) async-start(bf16[8,16,2048]{2,1,0:T(8,128)(2,1)} %bitcast.15), calls=%async_computation.3 | async-start | bytes 1048576 | tf_op jit(solution)/shard_map/all_to_all | solution.py:36
Sparse Core Ops, SparseCore 0:
  90.2 39.7 all-gather.1

commit v3 on v2

--- a/solution.py
+++ b/solution.py
@@ -9,8 +9,8 @@
 
 HD = 128
 KVH = 4
-BIG_VMEM = 60 * 1024 * 1024
-SMALL_VMEM = 24 * 1024 * 1024
+BIG_VMEM = 61 * 1024 * 1024
+SMALL_VMEM = 12 * 1024 * 1024
 AXES = ("exp", "rep", "tk")
 NX, NZL, NZH, NY = 4, 4, 2, 8
 NZ = NZL * NZH
@@ -49,8 +49,11 @@
     gain_ref,
     ids_ref,
     routing_ref,
+    previous_ref,
+    talker_gain_ref,
     sent_ref,
     residual_ref,
+    talker_ref,
 ):
     count, span, _ = keys_ref.shape
     width = hidden_ref.shape[1]
@@ -103,6 +106,10 @@
     for copy in range(sent_ref.shape[0]):
         sent_ref[copy, :, :width] = moe_in
         sent_ref[copy, :, width:] = route
+    previous = previous_ref[...].astype(jnp.float32)
+    norm = lax.rsqrt(jnp.mean(previous * previous, axis=-1, keepdims=True) + 1e-06)
+    gain = talker_gain_ref[...].astype(jnp.float32).reshape(1, width)
+    talker_ref[...] = (previous * norm * gain).astype(jnp.bfloat16)
 
 
 def origin(ndim, step):
@@ -122,6 +129,8 @@
     gain,
     ids,
     routing,
+    previous,
+    talker_gain,
 ):
     count, width = hidden.shape
     operands = (
@@ -134,6 +143,8 @@
         gain,
         ids.T,
         routing.T,
+        previous,
+        talker_gain,
     )
     return pl.pallas_call(
         attend_kernel,
@@ -143,127 +154,177 @@
         out_specs=[
             pl.BlockSpec((copies, count, width + experts), functools.partial(origin, 3)),
             pl.BlockSpec((count, width), functools.partial(origin, 2)),
+            pl.BlockSpec((count, width), functools.partial(origin, 2)),
         ],
         out_shape=[
             pltpu.HBM((copies, count, width + experts), jnp.bfloat16),
             jax.ShapeDtypeStruct((count, width), jnp.float32),
+            pltpu.HBM((count, width), jnp.bfloat16),
         ],
         compiler_params=pltpu.CompilerParams(vmem_limit_bytes=BIG_VMEM),
         name="attend",
     )(lengths, *operands)
 
 
-def slot_masks(route, slots):
-    rows, experts = route.shape
-    exp, rep, tk = (lax.axis_index(a) for a in AXES)
-    core, z_lo = rep % 2, exp % NZL
-    target = lax.broadcasted_iota(jnp.int32, (NX * NZ, experts), 0)
+def from_row(values, ahead):
+    return lax.ppermute(values, "tk", [((y + ahead) % NY, y) for y in range(NY)])
+
+
+def dispatch_kernel(where_ref, held_ref, o_ref, weight_ref, out_ref, sems):
+    core, tk, z_lo = where_ref[0], where_ref[1], where_ref[2]
+    width = o_ref.shape[1]
+    rows, experts = weight_ref.shape[0], held_ref.shape[1] - width
+    targets = NX * NZ
+    slots = weight_ref.shape[1] // targets
+    across = (((1,), (1,)), ((), ()))
+
+    def count(shape, axis):
+        return lax.broadcasted_iota(jnp.int32, shape, axis)
+
+    def bits(mask):
+        return mask.astype(jnp.bfloat16)
+
+    target = count((targets, experts), 0)
     x, rest = target // NZ, target % NZ
     holds = jnp.where(core == 0, (x * NZL + rest % NZL) * NY + tk, (x * NZL + z_lo) * NY + rest)
-    chosen = (holds == lax.broadcasted_iota(jnp.int32, holds.shape, 1)).astype(jnp.bfloat16)
-    share = lax.dot_general(
-        chosen, route, (((1,), (1,)), ((), ())), preferred_element_type=jnp.float32
-    )
-    member = share > 0
-    before = lax.broadcasted_iota(jnp.int32, (rows, rows), 0)
-    until = before <= lax.broadcasted_iota(jnp.int32, (rows, rows), 1)
-    rank = jnp.dot(
-        member.astype(jnp.bfloat16), until.astype(jnp.bfloat16), preferred_element_type=jnp.float32
-    ).astype(jnp.int32)
-    slot = lax.broadcasted_iota(jnp.int32, (target.shape[0], slots, rows), 1) + 1
-    inside = jnp.logical_and(member[:, None, :], rank[:, None, :] == slot)
-    pick = inside.astype(jnp.bfloat16).reshape(-1, rows)
-    weight = jnp.where(inside, share[:, None, :], 0.0).astype(jnp.bfloat16).reshape(-1, rows)
-    return pick, weight
-
-
-def weight_pieces(units, block):
-    pieces = []
-    for first in range(0, 2 * units, block):
-        for kind in range(2):
-            unit = first
-            while unit < first + block:
-                side, row = divmod(unit, units)
-                rows = min(first + block - unit, units - row)
-                place = 2 * first + kind * block + unit - first
-                pieces.append((2 * kind + side, row, rows, place))
-                unit += rows
-    return pieces
-
-
-def expert_kernel(x_ref, *refs):
-    weights, (o_ref, in_ref, down_ref, active_ref, out_ref, sems, out_sems) = refs[:6], refs[6:]
-    units = weights[0].shape[0]
-    block = 128
-    pieces = weight_pieces(units, block)
-    copies = [
-        pltpu.make_async_copy(
-            weights[array].at[pl.ds(row, rows)], in_ref.at[pl.ds(place, rows)], sems.at[i]
-        )
-        for i, (array, row, rows, place) in enumerate(pieces)
-    ]
-    down_copies = [
-        pltpu.make_async_copy(
-            weights[4 + i], down_ref.at[pl.ds(i * units, units)], sems.at[len(pieces) + i]
-        )
-        for i in range(2)
-    ]
-    for copy in copies + down_copies:
-        copy.start()
-    for first in range(0, 2 * units, block):
-        for copy, piece in zip(copies, pieces):
-            if 2 * first <= piece[3] < 2 * (first + block):
-                copy.wait()
-        both = lax.dot_general(
-            x_ref[...],
-            in_ref[2 * first : 2 * (first + block)],
-            (((1,), (1,)), ((), ())),
-            preferred_element_type=jnp.float32,
-        )
-        gated, raised = both[:, :block], both[:, block:]
-        active_ref[:, first : first + block] = (
-            gated / (1.0 + jnp.exp(-gated)) * raised
-        ).astype(jnp.bfloat16)
-    for copy in down_copies:
-        copy.wait()
+    chosen = bits(holds == count((targets, experts), 1))
+    route = held_ref[:, width:]
+
+    share = lax.dot_general(chosen, route, across, preferred_element_type=jnp.float32)
+    until = bits(count((rows, rows), 0) <= count((rows, rows), 1))
+    rank = jnp.dot(bits(share > 0), until, preferred_element_type=jnp.float32)
+    rank = jnp.where(share > 0, rank, 0.0)
+    shape = (targets, slots, rows)
+    slot = count(shape, 1).astype(jnp.float32) + 1.0
+    inside = jnp.broadcast_to(rank[:, None, :], shape) == slot
+    pick = bits(jnp.where(inside, 1.0, 0.0).reshape(targets * slots, rows))
     parts, _, part = out_ref.shape
-    out_copies = []
+    copies = []
     for i in range(parts):
         lanes = pl.ds(i * part, part)
-        out = jnp.dot(active_ref[...], down_ref[:, lanes], preferred_element_type=jnp.float32)
+        out = jnp.dot(pick, held_ref[:, lanes], preferred_element_type=jnp.float32)
         out_ref[i] = out.astype(jnp.bfloat16)
-        out_copies.append(pltpu.make_async_copy(out_ref.at[i], o_ref.at[:, lanes], out_sems.at[i]))
-        out_copies[-1].start()
-    for copy in out_copies:
+        copies.append(pltpu.make_async_copy(out_ref.at[i], o_ref.at[:, lanes], sems.at[i]))
+        copies[-1].start()
+
+    share = lax.dot_general(route, chosen, across, preferred_element_type=jnp.float32)
+    since = bits(count((rows, rows), 0) >= count((rows, rows), 1))
+    rank = jnp.dot(since, bits(share > 0), preferred_element_type=jnp.float32)
+    rank = jnp.where(share > 0, rank, 0.0)
+    wide = (targets, targets * slots)
+    repeat = bits(count(wide, 0) == count(wide, 1) // slots)
+    rank = jnp.dot(rank.astype(jnp.bfloat16), repeat, preferred_element_type=jnp.float32)
+    share = jnp.dot(share.astype(jnp.bfloat16), repeat, preferred_element_type=jnp.float32)
+    slot = (count(rank.shape, 1) % slots).astype(jnp.float32) + 1.0
+    weight_ref[...] = jnp.where(rank == slot, share, 0.0).astype(jnp.bfloat16)
+    for copy in copies:
         copy.wait()
 
 
-def expert_apply(rows, weights):
+def dispatch(held, width, slots):
+    rows = held.shape[0]
+    count = NX * NZ * slots
+    exp, rep, tk = (lax.axis_index(a) for a in AXES)
+    where = jnp.stack([rep % 2, tk, exp % NZL]).astype(jnp.int32)
+    parts = 4
+    return pl.pallas_call(
+        dispatch_kernel,
+        in_specs=[
+            pl.BlockSpec(memory_space=pltpu.SMEM),
+            pl.BlockSpec(memory_space=pltpu.VMEM),
+        ],
+        out_specs=[
+            pl.BlockSpec(memory_space=pltpu.HBM),
+            pl.BlockSpec(memory_space=pltpu.VMEM),
+        ],
+        out_shape=[
+            pltpu.HBM((count, width), jnp.bfloat16),
+            jax.ShapeDtypeStruct((rows, count), jnp.bfloat16),
+        ],
+        scratch_shapes=[
+            pltpu.VMEM((parts, count, width // parts), jnp.bfloat16),
+            pltpu.SemaphoreType.DMA((parts,)),
+        ],
+        compiler_params=pltpu.CompilerParams(vmem_limit_bytes=SMALL_VMEM),
+        name="dispatch",
+    )(where, held)
+
+
+def pack_kernel(*refs):
+    weights, (packed_ref, sems) = refs[:-2], refs[-2:]
+    units = weights[0].shape[0]
+    copies = [
+        pltpu.make_async_copy(w, packed_ref.at[pl.ds(i * units, units)], sems.at[i])
+        for i, w in enumerate(weights)
+    ]
+    for copy in copies:
+        copy.start()
+    for copy in copies:
+        copy.wait()
+
+
+def pack(weights):
+    units, width = weights[0].shape
+    count = len(weights)
+    return pl.pallas_call(
+        pack_kernel,
+        in_specs=[pl.BlockSpec(memory_space=pl.ANY)] * count,
+        out_specs=pl.BlockSpec(memory_space=pltpu.HBM),
+        out_shape=pltpu.HBM((count * units, width), jnp.bfloat16),
+        scratch_shapes=[pltpu.SemaphoreType.DMA((count,))],
+        compiler_params=pltpu.CompilerParams(vmem_limit_bytes=SMALL_VMEM),
+        cost_estimate=pl.CostEstimate(
+            flops=0, bytes_accessed=4 * count * units * width, transcendentals=0
+        ),
+        name="pack",
+    )(*weights)
+
+
+def expert_kernel(x_ref, packed_ref, o_ref, out_ref, sems):
+    units = packed_ref.shape[0] // 3
+    both = lax.dot_general(
+        x_ref[...],
+        packed_ref[: 2 * units],
+        (((1,), (1,)), ((), ())),
+        preferred_element_type=jnp.float32,
+    )
+    gated, raised = both[:, :units], both[:, units:]
+    active = (gated / (1.0 + jnp.exp(-gated)) * raised).astype(jnp.bfloat16)
+    parts, _, part = out_ref.shape
+    copies = []
+    for i in range(parts):
+        lanes = pl.ds(i * part, part)
+        out = jnp.dot(
+            active, packed_ref[2 * units :, lanes], preferred_element_type=jnp.float32
+        )
+        out_ref[i] = out.astype(jnp.bfloat16)
+        copies.append(pltpu.make_async_copy(out_ref.at[i], o_ref.at[:, lanes], sems.at[i]))
+        copies[-1].start()
+    for copy in copies:
+        copy.wait()
+
+
+def expert_apply(rows, packed):
     count, width = rows.shape
-    units = weights[0].shape[0]
+    units = packed.shape[0] // 3
     parts = 4
     return pl.pallas_call(
         expert_kernel,
-        in_specs=[pl.BlockSpec(memory_space=pltpu.VMEM)]
-        + [pl.BlockSpec(memory_space=pltpu.HBM)] * 6,
+        in_specs=[pl.BlockSpec(memory_space=pltpu.VMEM)] * 2,
         out_specs=pl.BlockSpec(memory_space=pltpu.HBM),
         out_shape=pltpu.HBM((count, width), jnp.bfloat16),
         scratch_shapes=[
-            pltpu.VMEM((4 * units, width), jnp.bfloat16),
-            pltpu.VMEM((2 * units, width), jnp.bfloat16),
-            pltpu.VMEM((count, 2 * units), jnp.bfloat16),
             pltpu.VMEM((parts, count, width // parts), jnp.bfloat16),
-            pltpu.SemaphoreType.DMA((16,)),
             pltpu.SemaphoreType.DMA((parts,)),
         ],
         compiler_params=pltpu.CompilerParams(vmem_limit_bytes=SMALL_VMEM),
         cost_estimate=pl.CostEstimate(
-            flops=12 * count * width * units,
-            bytes_accessed=4 * count * width + 12 * units * width,
-            transcendentals=2 * count * units,
+            flops=6 * count * width * units,
+            bytes_accessed=4 * count * width + 6 * units * width,
+            transcendentals=count * units,
         ),
         name="experts",
-    )(rows, *weights)
+    )(rows, packed)
 
 
 def per_device(
@@ -289,7 +350,7 @@
     lines, planes = line_groups(), plane_groups()
     line = len(lines[0])
 
-    sent, residual = attend(
+    sent, residual, talker_rows = attend(
         line,
         experts,
         hidden_input_rows,
@@ -302,34 +363,46 @@
         moe_gain,
         expert_ids,
         routing_weights,
-    )
-
-    wide = prev_hidden.astype(jnp.float32)
-    unit = wide * lax.rsqrt(jnp.mean(wide * wide, axis=-1, keepdims=True) + 1e-06)
-    talker_units = lax.all_gather(unit, "tk", axis=0, tiled=True)
+        prev_hidden,
+        talker_gain,
+    )
+
+    near = [from_row(talker_rows, 1), from_row(talker_rows, -1)]
+    held = exchange(sent, lines).reshape(line * count, width + experts)
+    held, near = lax.optimization_barrier((held, near))
+    slots = 2 * line
+    outgoing, weight = dispatch(held, width, slots)
 
     own = [w[0].T for w in (expert_gate, expert_up, expert_down)]
-    sent, own = lax.optimization_barrier((sent, own))
+    outgoing, own, near = lax.optimization_barrier((outgoing, own, near))
     other = [lax.ppermute(w, "rep", [(r, r ^ 1) for r in range(2 * NZH)]) for w in own]
-    held = exchange(sent, lines).reshape(line * count, width + experts)
-    held, own, other = lax.optimization_barrier((held, own, other))
-    slots = 2 * line
-    pick, weight = slot_masks(held[:, width:], slots)
-    outgoing = jnp.dot(pick, held[:, :width], preferred_element_type=jnp.float32)
-    outgoing = outgoing.astype(jnp.bfloat16).reshape(-1, slots, width)
-    arrived = exchange(outgoing, planes).reshape(-1, width)
-    weights = [own[0], other[0], own[1], other[1], own[2], other[2]]
-    computed = expert_apply(arrived, weights)
+    second = [from_row(near[0], 1), from_row(near[1], -1)]
+    arrived = exchange(outgoing.reshape(-1, slots, width), planes).reshape(-1, width)
+    packed = pack([own[0], other[0], own[1], other[1], own[2], other[2]])
+    arrived, packed, second = lax.optimization_barrier((arrived, packed, second))
+    computed = expert_apply(arrived, packed)
+
+    computed, second = lax.optimization_barrier((computed, second))
+    third = [from_row(second[0], 1), from_row(second[1], -1)]
+    half = count // 2
+    third += [from_row(second[0][:half], 2), from_row(second[1][half:], -2)]
     returned = exchange(computed.reshape(-1, slots, width), planes).reshape(-1, width)
-    partial_rows = lax.dot_general(
-        weight, returned, (((0,), (0,)), ((), ())), preferred_element_type=jnp.float32
-    ).astype(jnp.bfloat16)
+    returned, third = lax.optimization_barrier((returned, third))
+    partial_rows = jnp.dot(weight, returned, preferred_element_type=jnp.float32)
+    partial_rows = partial_rows.astype(jnp.bfloat16)
+    partial_rows, third = lax.optimization_barrier((partial_rows, third))
     pieces = exchange(partial_rows.reshape(line, count, width), lines)
     layer_out = (residual + jnp.sum(pieces.astype(jnp.float32), axis=0)).astype(jnp.bfloat16)
 
-    talker_rows = (talker_units * talker_gain.astype(jnp.float32)).astype(jnp.bfloat16)
-    talker_in = jnp.dot(talker_rows, talker_proj, preferred_element_type=jnp.float32)
-    return (layer_out, talker_in.astype(jnp.bfloat16))
+    ahead = [talker_rows, near[0], second[0], third[0], third[2], third[3]]
+    gathered = jnp.concatenate(ahead + [third[1], second[1], near[1]], axis=0)
+    talker_in = jnp.dot(gathered, talker_proj, preferred_element_type=jnp.float32)
+    talker_in = talker_in.astype(jnp.bfloat16)
+    start = (NY - lax.axis_index("tk")) * count
+    talker_in = lax.dynamic_slice_in_dim(
+        jnp.concatenate([talker_in, talker_in], axis=0), start, NY * count, axis=0
+    )
+    return (layer_out, talker_in)
 
 
 def solution(mesh):

time: 144 us -> 135 us (0.938)
  blocking collectives: 36.8 us -> 0 us
  starting transfers between devices: 27.9 us -> 64.6 us
  between operations: 14.3 us -> 0.9 us
  local copies, waits for them, and re-layouts: 0.12 us -> 12.6 us
  waiting for transfers between devices: 46 us -> 36.5 us
  Pallas kernels: 11.4 us -> 14.2 us
  matrix products: 4.53 us -> 2.59 us
    all_to_all x1 -> x0, blocking collectives: 36.8 us -> none  [exchange(): lax.all_to_all(blocks, AXES, split_axis=0, concat_axis=0, axis_index_grou...]
    all_to_all x3 -> x4, waiting for transfers between devices: 36.8 us -> 9.41 us  [exchange(): lax.all_to_all(blocks, AXES, split_axis=0, concat_axis=0, axis_index_grou...]
    ppermute x0 -> x8, waiting for transfers between devices: none -> 27.1 us  [from_row(): lax.ppermute(values, 'tk', [((y + ahead) % NY, y) for y in range(NY)])]
    ppermute x0 -> x8, starting transfers between devices: none -> 24.7 us  [from_row(): lax.ppermute(values, 'tk', [((y + ahead) % NY, y) for y in range(NY)])]
    unnamed x14 -> x26, local copies, waits for them, and re-layouts: 0.04 us -> 12 us
    all_to_all x3 -> x4, starting transfers between devices: 21.6 us -> 30.5 us  [exchange(): lax.all_to_all(blocks, AXES, split_axis=0, concat_axis=0, axis_index_grou...]
    all_gather x1 -> x0, waiting for transfers between devices: 6.9 us -> none  [per_device(): talker_units = lax.all_gather(unit, 'tk', axis=0, tiled=True)]
    pallas_call x0 -> x2, Pallas kernels: none -> 4.73 us  [the longest x1 2.54 us: dispatch(): pl.pallas_call(dispatch_kernel, in_specs=[pl.BlockSpec(memory_space=pltpu...]
  transfers between devices with their start and end apart: 7 -> 15, of which waited for: 5 -> 8; matrix products, arithmetic and copies ran while one was open for 3% -> 6% of each run, Pallas kernels for 0% -> 2%
where the time goes in v3:
time: 135 us; the launch traced here: 133 us
  starting transfers between devices  64.6 us (48%)
  waiting for transfers between devices  36.5 us (27%)
  Pallas kernels  14.2 us (11%)
  local copies, waits for them, and re-layouts  12.6 us (9%)
  matrix products  2.59 us (2%)
  other arithmetic  1.53 us (1%)
    all_to_all x4, starting transfers between devices, exchange(): lax.all_to_all(blocks, AXES, split_axis=0, concat_axis=0, axis_index_grou...  30.5 us
    ppermute x8, waiting for transfers between devices, from_row(): lax.ppermute(values, 'tk', [((y + ahead) % NY, y) for y in range(NY)])  27.1 us
    ppermute x8, starting transfers between devices, from_row(): lax.ppermute(values, 'tk', [((y + ahead) % NY, y) for y in range(NY)])  24.7 us
    unnamed x26, local copies, waits for them, and re-layouts  12 us
    ppermute x3, starting transfers between devices, per_device(): lax.ppermute(w, 'rep', [(r, r ^ 1) for r in range(2 * NZH)])  9.44 us
    all_to_all x4, waiting for transfers between devices, exchange(): lax.all_to_all(blocks, AXES, split_axis=0, concat_axis=0, axis_index_grou...  9.41 us
    pallas_call x1, Pallas kernels, expert_apply(): pl.pallas_call(expert_kernel, in_specs=[pl.BlockSpec(memory_space=pltpu.V...  4.89 us
    pallas_call x1, Pallas kernels, attend(): pl.pallas_call(attend_kernel, grid=(1,), in_specs=[pl.BlockSpec(memory_sp...  4.55 us
  transfers between devices with their start and end apart: 15, of which 8 were waited for; matrix products, arithmetic and copies ran while one was open for 6% of the time, Pallas kernels for 2%

profile of v3, /device:TPU:1, one launch (start us, length us, event | category | flops | bytes accessed | tf_op | source)
XLA Modules:
  0.0 132.9 jit_solution(8236098235943037041)
XLA Ops:
  0.7 4.5 %attend.1 = (bf16[8,16,2176]{2,1,0:T(8,128)(2,1)}, f32[16,2048]{1,0:T(8,128)}, bf16[16,2048]{1,0:T(8,128)(2,1)}) custom-call(s32[16]{0:T(128)} %lengths_ref.1, bf16[16,2048]{1,0:T(8,128)(2,1)} %hidden_ref.1, bf16[16,2048]{1,0:T(8,128)(2,1)} %q_ref.1, bf16[16,512]{1,0:T(8,128)(2,1)} %new_key_ref.1, bf16[16,512]{1,0:T(8,128)(2,1)} %new_value_ref.1, ...), custom_call_target="tpu_custom_call" | custom-call | tf_op jit(solution)/shard_map/attend/pallas_call | solution.py:149
  5.2 10.9 %all-to-all-start = ((bf16[8,16,2176]{2,1,0:T(8,128)(2,1)}), bf16[8,16,2176]{2,1,0:T(8,128)(2,1)S(1)}, u32[]{:S(2)}, u32[]{:S(2)}) async-start(bf16[8,16,2176]{2,1,0:T(8,128)(2,1)} %get-tuple-element.34), calls=%async_computation | async-start | bytes 1114112 | tf_op jit(solution)/shard_map/all_to_all | solution.py:36
  16.1 5.1 %collective-permute-start = (bf16[16,2048]{1,0:T(8,128)(2,1)}, bf16[16,2048]{1,0:T(8,128)(2,1)}, u32[]{:S(2)}, u32[]{:S(2)}) collective-permute-start(bf16[16,2048]{1,0:T(8,128)(2,1)} %get-tuple-element.35), channel_id=1, source_target_pairs={{1,0},{2,1},{3,2},{4,3},{5,4},{6,5},{7,6},{0,7},{9,8},{10,9},{11,1... | collective-permute-start | bytes 196616 | tf_op jit(solution)/shard_map/ppermute | solution.py:170
  21.2 1.9 %collective-permute-start.1 = (bf16[16,2048]{1,0:T(8,128)(2,1)}, bf16[16,2048]{1,0:T(8,128)(2,1)S(1)}, u32[]{:S(2)}, u32[]{:S(2)}) collective-permute-start(bf16[16,2048]{1,0:T(8,128)(2,1)} %get-tuple-element.35), channel_id=1, source_target_pairs={{7,0},{0,1},{1,2},{2,3},{3,4},{4,5},{5,6},{6,7},{15,8},{8,9},{9,10... | collective-permute-start | bytes 196616 | tf_op jit(solution)/shard_map/ppermute | solution.py:170
  23.2 2.0 %collective-permute-done = bf16[16,2048]{1,0:T(8,128)(2,1)} collective-permute-done((bf16[16,2048]{1,0:T(8,128)(2,1)}, bf16[16,2048]{1,0:T(8,128)(2,1)}, u32[]{:S(2)}, u32[]{:S(2)}) %collective-permute-start) | collective-permute-done | bytes 65568 | tf_op jit(solution)/shard_map/ppermute | solution.py:170
  25.2 4.2 %collective-permute-done.1 = bf16[16,2048]{1,0:T(8,128)(2,1)S(1)} collective-permute-done((bf16[16,2048]{1,0:T(8,128)(2,1)}, bf16[16,2048]{1,0:T(8,128)(2,1)S(1)}, u32[]{:S(2)}, u32[]{:S(2)}) %collective-permute-start.1) | collective-permute-done | bytes 65568 | tf_op jit(solution)/shard_map/ppermute | solution.py:170
  29.3 2.5 %dispatch.1 = (bf16[512,2048]{1,0:T(8,128)(2,1)}, bf16[128,512]{1,0:T(8,128)(2,1)S(1)}) custom-call(s32[3]{0:T(128)S(1)} %pad_add_fusion.where_ref, bf16[128,2176]{1,0:T(8,128)(2,1)S(1)} %bitcast.24), custom_call_target="tpu_custom_call" | custom-call | tf_op jit(solution)/shard_map/dispatch/pallas_call | solution.py:230
  31.9 8.9 %all-to-all-start.1 = ((bf16[32,16,2048]{2,1,0:T(8,128)(2,1)}), bf16[32,16,2048]{2,1,0:T(8,128)(2,1)S(1)}, u32[]{:S(2)}, u32[]{:S(2)}) async-start(bf16[32,16,2048]{2,1,0:T(8,128)(2,1)} %bitcast.34), calls=%async_computation.1 | async-start | bytes 4194304 | tf_op jit(solution)/shard_map/all_to_all | solution.py:36
  40.8 5.1 %collective-permute-start.2 = (bf16[192,2048]{1,0:T(8,128)(2,1)}, bf16[192,2048]{1,0:T(8,128)(2,1)S(1)}, u32[]{:S(2)}, u32[]{:S(2)}) collective-permute-start(bf16[192,2048]{1,0:T(8,128)(2,1)} %bitcast.26), channel_id=1, source_target_pairs={{0,8},{8,0},{16,24},{24,16},{1,9},{9,1},{17,25},{25,17},{2,10},{10... | collective-permute-start | bytes 2359304 | tf_op jit(solution)/shard_map/ppermute | solution.py:378
  45.9 1.9 %collective-permute-start.3 = (bf16[192,2048]{1,0:T(8,128)(2,1)}, bf16[192,2048]{1,0:T(8,128)(2,1)S(1)}, u32[]{:S(2)}, u32[]{:S(2)}) collective-permute-start(bf16[192,2048]{1,0:T(8,128)(2,1)} %bitcast.28), channel_id=1, source_target_pairs={{0,8},{8,0},{16,24},{24,16},{1,9},{9,1},{17,25},{25,17},{2,10},{10... | collective-permute-start | bytes 2359304 | tf_op jit(solution)/shard_map/ppermute | solution.py:378
  47.8 2.4 %collective-permute-start.4 = (bf16[192,2048]{1,0:T(8,128)(2,1)}, bf16[192,2048]{1,0:T(8,128)(2,1)S(1)}, u32[]{:S(2)}, u32[]{:S(2)}) collective-permute-start(bf16[192,2048]{1,0:T(8,128)(2,1)} %bitcast.30), channel_id=1, source_target_pairs={{0,8},{8,0},{16,24},{24,16},{1,9},{9,1},{17,25},{25,17},{2,10},{10... | collective-permute-start | bytes 2359304 | tf_op jit(solution)/shard_map/ppermute | solution.py:378
  50.3 1.9 %collective-permute-start.5 = (bf16[16,2048]{1,0:T(8,128)(2,1)}, bf16[16,2048]{1,0:T(8,128)(2,1)S(1)}, u32[]{:S(2)}, u32[]{:S(2)}) collective-permute-start(bf16[16,2048]{1,0:T(8,128)(2,1)} %collective-permute-done), channel_id=1, source_target_pairs={{1,0},{2,1},{3,2},{4,3},{5,4},{6,5},{7,6},{0,7},{9,8},{10,9},{11,1... | collective-permute-start | bytes 196616 | tf_op jit(solution)/shard_map/ppermute | solution.py:170
  52.2 3.4 %collective-permute-start.6 = (bf16[16,2048]{1,0:T(8,128)(2,1)S(1)}, bf16[16,2048]{1,0:T(8,128)(2,1)S(1)}, u32[]{:S(2)}, u32[]{:S(2)}) collective-permute-start(bf16[16,2048]{1,0:T(8,128)(2,1)S(1)} %collective-permute-done.1), channel_id=1, source_target_pairs={{7,0},{0,1},{1,2},{2,3},{3,4},{4,5},{5,6},{6,7},{15,8},{8,9},{9,10... | collective-permute-start | bytes 196616 | tf_op jit(solution)/shard_map/ppermute | solution.py:170
  56.7 1.1 copy-done.3
  57.9 1.1 copy-done.4
  59.0 2.2 %pack.1.packed_ref = bf16[1152,2048]{1,0:T(8,128)(2,1)} custom-call(bf16[192,2048]{1,0:T(8,128)(2,1)S(1)} %bitcast.27, bf16[192,2048]{1,0:T(8,128)(2,1)S(1)} %collective-permute-done.2.refs_1_, bf16[192,2048]{1,0:T(8,128)(2,1)S(1)} %bitcast.29, bf16[192,2048]{1,0:T(8,128)(2,1)S(1)} %collective-permute-done.3.refs_3_, bf16[192,2048]{1,0:T(8,128)(2,1)S(1)} %bitcast.31, ...), custom_call_target="tpu_custom_call" | custom-call | bytes 9437184 | tf_op jit(solution)/shard_map/pack/pallas_call | solution.py:269
  61.2 6.1 %collective-permute-done.5 = bf16[16,2048]{1,0:T(8,128)(2,1)S(1)} collective-permute-done((bf16[16,2048]{1,0:T(8,128)(2,1)}, bf16[16,2048]{1,0:T(8,128)(2,1)S(1)}, u32[]{:S(2)}, u32[]{:S(2)}) %collective-permute-start.5) | collective-permute-done | bytes 65568 | tf_op jit(solution)/shard_map/ppermute | solution.py:170
  67.3 2.9 %all-to-all-done.1 = bf16[32,16,2048]{2,1,0:T(8,128)(2,1)S(1)} async-done(((bf16[32,16,2048]{2,1,0:T(8,128)(2,1)}), bf16[32,16,2048]{2,1,0:T(8,128)(2,1)S(1)}, u32[]{:S(2)}, u32[]{:S(2)}) %all-to-all-start.1) | async-done | bytes 2097184 | tf_op jit(solution)/shard_map/all_to_all | solution.py:36
  70.2 2.3 %copy-done.1 = bf16[1152,2048]{1,0:T(8,128)(2,1)S(1)} copy-done((bf16[1152,2048]{1,0:T(8,128)(2,1)S(1)}, bf16[1152,2048]{1,0:T(8,128)(2,1)}, u32[]{:S(2)}) %copy-start.1) | copy-done | bytes 4718616
  72.5 4.9 %experts.1 = bf16[512,2048]{1,0:T(8,128)(2,1)} custom-call(bf16[512,2048]{1,0:T(8,128)(2,1)S(1)} %bitcast.25, bf16[1152,2048]{1,0:T(8,128)(2,1)S(1)} %copy-done.1), custom_call_target="tpu_custom_call" | custom-call | flops 2415919104 | bytes 8912896 | tf_op jit(solution)/shard_map/experts/pallas_call | solution.py:311
  77.4 6.7 %all-to-all-start.2 = ((bf16[32,16,2048]{2,1,0:T(8,128)(2,1)}), bf16[32,16,2048]{2,1,0:T(8,128)(2,1)S(1)}, u32[]{:S(2)}, u32[]{:S(2)}) async-start(bf16[32,16,2048]{2,1,0:T(8,128)(2,1)} %bitcast.33), calls=%async_computation.2 | async-start | bytes 4194304 | tf_op jit(solution)/shard_map/all_to_all | solution.py:36
  85.8 4.3 %collective-permute-start.7 = (bf16[16,2048]{1,0:T(8,128)(2,1)S(1)}, bf16[16,2048]{1,0:T(8,128)(2,1)S(1)}, u32[]{:S(2)}, u32[]{:S(2)}) collective-permute-start(bf16[16,2048]{1,0:T(8,128)(2,1)S(1)} %collective-permute-done.5), channel_id=1, source_target_pairs={{1,0},{2,1},{3,2},{4,3},{5,4},{6,5},{7,6},{0,7},{9,8},{10,9},{11,1... | collective-permute-start | bytes 196616 | tf_op jit(solution)/shard_map/ppermute | solution.py:170
  90.2 1.9 %collective-permute-start.8 = (bf16[16,2048]{1,0:T(8,128)(2,1)S(1)}, bf16[16,2048]{1,0:T(8,128)(2,1)}, u32[]{:S(2)}, u32[]{:S(2)}) collective-permute-start(bf16[16,2048]{1,0:T(8,128)(2,1)S(1)} %collective-permute-done.6), channel_id=1, source_target_pairs={{7,0},{0,1},{1,2},{2,3},{3,4},{4,5},{5,6},{6,7},{15,8},{8,9},{9,10... | collective-permute-start | bytes 196616 | tf_op jit(solution)/shard_map/ppermute | solution.py:170
  92.1 4.3 %collective-permute-start.9 = (bf16[8,2048]{1,0:T(8,128)(2,1)S(1)}, bf16[8,2048]{1,0:T(8,128)(2,1)S(1)}, u32[]{:S(2)}, u32[]{:S(2)}) collective-permute-start(bf16[8,2048]{1,0:T(8,128)(2,1)S(1)} %slice.6), channel_id=1, source_target_pairs={{2,0},{3,1},{4,2},{5,3},{6,4},{7,5},{0,6},{1,7},{10,8},{11,9},{12,... | collective-permute-start | bytes 98312 | tf_op jit(solution)/shard_map/ppermute | solution.py:170
  96.4 1.9 %collective-permute-start.10 = (bf16[8,2048]{1,0:T(8,128)(2,1)S(1)}, bf16[8,2048]{1,0:T(8,128)(2,1)S(1)}, u32[]{:S(2)}, u32[]{:S(2)}) collective-permute-start(bf16[8,2048]{1,0:T(8,128)(2,1)S(1)} %slice.7), channel_id=1, source_target_pairs={{6,0},{7,1},{0,2},{1,3},{2,4},{3,5},{4,6},{5,7},{14,8},{15,9},{8,1... | collective-permute-start | bytes 98312 | tf_op jit(solution)/shard_map/ppermute | solution.py:170
  98.3 13.1 %collective-permute-done.9 = bf16[8,2048]{1,0:T(8,128)(2,1)S(1)} collective-permute-done((bf16[8,2048]{1,0:T(8,128)(2,1)S(1)}, bf16[8,2048]{1,0:T(8,128)(2,1)S(1)}, u32[]{:S(2)}, u32[]{:S(2)}) %collective-permute-start.9) | collective-permute-done | bytes 32800 | tf_op jit(solution)/shard_map/ppermute | solution.py:170
  111.4 1.7 %collective-permute-done.10 = bf16[8,2048]{1,0:T(8,128)(2,1)S(1)} collective-permute-done((bf16[8,2048]{1,0:T(8,128)(2,1)S(1)}, bf16[8,2048]{1,0:T(8,128)(2,1)S(1)}, u32[]{:S(2)}, u32[]{:S(2)}) %collective-permute-start.10) | collective-permute-done | bytes 32800 | tf_op jit(solution)/shard_map/ppermute | solution.py:170
  114.5 1.3 convolution_convert_fusion
  115.8 4.0 %all-to-all-start.3 = ((bf16[8,16,2048]{2,1,0:T(8,128)(2,1)}), bf16[8,16,2048]{2,1,0:T(8,128)(2,1)S(1)}, u32[]{:S(2)}, u32[]{:S(2)}) async-start(bf16[8,16,2048]{2,1,0:T(8,128)(2,1)} %bitcast.35), calls=%async_computation.3 | async-start | bytes 1048576 | tf_op jit(solution)/shard_map/all_to_all | solution.py:36
  121.6 1.5 %constant_dynamic-update-slice_fusion.2 = bf16[128,2048]{1,0:T(8,128)(2,1)} fusion(bf16[128,2048]{1,0:T(8,128)(2,1)} %constant_dynamic-update-slice_fusion.3, bf16[16,2048]{1,0:T(8,128)(2,1)} %collective-permute-done.8), kind=kLoop, calls=%fused_computation.9 | loop fusion | bytes 131072
  124.3 1.3 convolution_convert_fusion.1
  126.4 5.8 %all-to-all-done.3 = bf16[8,16,2048]{2,1,0:T(8,128)(2,1)S(1)} async-done(((bf16[8,16,2048]{2,1,0:T(8,128)(2,1)}), bf16[8,16,2048]{2,1,0:T(8,128)(2,1)S(1)}, u32[]{:S(2)}, u32[]{:S(2)}) %all-to-all-start.3) | async-done | bytes 524320 | tf_op jit(solution)/shard_map/all_to_all | solution.py:36
  (37 shorter events, 8.8 us)
Async XLA Ops:
  0.6 123.7 %copy-start = (bf16[2048,128]{1,0:T(8,128)(2,1)S(1)}, bf16[2048,128]{1,0:T(8,128)(2,1)}, u32[]{:S(2)}) copy-start(bf16[2048,128]{1,0:T(8,128)(2,1)} %param.31) | copy-start | bytes 1572868
  5.2 24.1 %all-to-all-start = ((bf16[8,16,2176]{2,1,0:T(8,128)(2,1)}), bf16[8,16,2176]{2,1,0:T(8,128)(2,1)S(1)}, u32[]{:S(2)}, u32[]{:S(2)}) async-start(bf16[8,16,2176]{2,1,0:T(8,128)(2,1)} %get-tuple-element.34), calls=%async_computation | async-start | bytes 1114112 | tf_op jit(solution)/shard_map/all_to_all | solution.py:36
  16.1 9.1 %collective-permute-start = (bf16[16,2048]{1,0:T(8,128)(2,1)}, bf16[16,2048]{1,0:T(8,128)(2,1)}, u32[]{:S(2)}, u32[]{:S(2)}) collective-permute-start(bf16[16,2048]{1,0:T(8,128)(2,1)} %get-tuple-element.35), channel_id=1, source_target_pairs={{1,0},{2,1},{3,2},{4,3},{5,4},{6,5},{7,6},{0,7},{9,8},{10,9},{11,1... | collective-permute-start | bytes 196616 | tf_op jit(solution)/shard_map/ppermute | solution.py:170
  21.2 8.2 %collective-permute-start.1 = (bf16[16,2048]{1,0:T(8,128)(2,1)}, bf16[16,2048]{1,0:T(8,128)(2,1)S(1)}, u32[]{:S(2)}, u32[]{:S(2)}) collective-permute-start(bf16[16,2048]{1,0:T(8,128)(2,1)} %get-tuple-element.35), channel_id=1, source_target_pairs={{7,0},{0,1},{1,2},{2,3},{3,4},{4,5},{5,6},{6,7},{15,8},{8,9},{9,10... | collective-permute-start | bytes 196616 | tf_op jit(solution)/shard_map/ppermute | solution.py:170
  31.9 38.3 %all-to-all-start.1 = ((bf16[32,16,2048]{2,1,0:T(8,128)(2,1)}), bf16[32,16,2048]{2,1,0:T(8,128)(2,1)S(1)}, u32[]{:S(2)}, u32[]{:S(2)}) async-start(bf16[32,16,2048]{2,1,0:T(8,128)(2,1)} %bitcast.34), calls=%async_computation.1 | async-start | bytes 4194304 | tf_op jit(solution)/shard_map/all_to_all | solution.py:36
  40.8 14.8 %collective-permute-start.2 = (bf16[192,2048]{1,0:T(8,128)(2,1)}, bf16[192,2048]{1,0:T(8,128)(2,1)S(1)}, u32[]{:S(2)}, u32[]{:S(2)}) collective-permute-start(bf16[192,2048]{1,0:T(8,128)(2,1)} %bitcast.26), channel_id=1, source_target_pairs={{0,8},{8,0},{16,24},{24,16},{1,9},{9,1},{17,25},{25,17},{2,10},{10... | collective-permute-start | bytes 2359304 | tf_op jit(solution)/shard_map/ppermute | solution.py:378
  45.9 9.7 %collective-permute-start.3 = (bf16[192,2048]{1,0:T(8,128)(2,1)}, bf16[192,2048]{1,0:T(8,128)(2,1)S(1)}, u32[]{:S(2)}, u32[]{:S(2)}) collective-permute-start(bf16[192,2048]{1,0:T(8,128)(2,1)} %bitcast.28), channel_id=1, source_target_pairs={{0,8},{8,0},{16,24},{24,16},{1,9},{9,1},{17,25},{25,17},{2,10},{10... | collective-permute-start | bytes 2359304 | tf_op jit(solution)/shard_map/ppermute | solution.py:378
  47.8 7.7 %collective-permute-start.4 = (bf16[192,2048]{1,0:T(8,128)(2,1)}, bf16[192,2048]{1,0:T(8,128)(2,1)S(1)}, u32[]{:S(2)}, u32[]{:S(2)}) collective-permute-start(bf16[192,2048]{1,0:T(8,128)(2,1)} %bitcast.30), channel_id=1, source_target_pairs={{0,8},{8,0},{16,24},{24,16},{1,9},{9,1},{17,25},{25,17},{2,10},{10... | collective-permute-start | bytes 2359304 | tf_op jit(solution)/shard_map/ppermute | solution.py:378
  50.3 17.0 %collective-permute-start.5 = (bf16[16,2048]{1,0:T(8,128)(2,1)}, bf16[16,2048]{1,0:T(8,128)(2,1)S(1)}, u32[]{:S(2)}, u32[]{:S(2)}) collective-permute-start(bf16[16,2048]{1,0:T(8,128)(2,1)} %collective-permute-done), channel_id=1, source_target_pairs={{1,0},{2,1},{3,2},{4,3},{5,4},{6,5},{7,6},{0,7},{9,8},{10,9},{11,1... | collective-permute-start | bytes 196616 | tf_op jit(solution)/shard_map/ppermute | solution.py:170
  52.2 15.1 %collective-permute-start.6 = (bf16[16,2048]{1,0:T(8,128)(2,1)S(1)}, bf16[16,2048]{1,0:T(8,128)(2,1)S(1)}, u32[]{:S(2)}, u32[]{:S(2)}) collective-permute-start(bf16[16,2048]{1,0:T(8,128)(2,1)S(1)} %collective-permute-done.1), channel_id=1, source_target_pairs={{7,0},{0,1},{1,2},{2,3},{3,4},{4,5},{5,6},{6,7},{15,8},{8,9},{9,10... | collective-permute-start | bytes 196616 | tf_op jit(solution)/shard_map/ppermute | solution.py:170
  55.6 1.1 copy-start.2
  56.7 1.1 copy-start.3
  57.9 1.1 copy-start.4
  70.2 2.3 %copy-start.1 = (bf16[1152,2048]{1,0:T(8,128)(2,1)S(1)}, bf16[1152,2048]{1,0:T(8,128)(2,1)}, u32[]{:S(2)}) copy-start(bf16[1152,2048]{1,0:T(8,128)(2,1)} %pack.1.packed_ref) | copy-start | bytes 14155780
  77.4 37.1 %all-to-all-start.2 = ((bf16[32,16,2048]{2,1,0:T(8,128)(2,1)}), bf16[32,16,2048]{2,1,0:T(8,128)(2,1)S(1)}, u32[]{:S(2)}, u32[]{:S(2)}) async-start(bf16[32,16,2048]{2,1,0:T(8,128)(2,1)} %bitcast.33), calls=%async_computation.2 | async-start | bytes 4194304 | tf_op jit(solution)/shard_map/all_to_all | solution.py:36
  85.8 27.4 %collective-permute-start.7 = (bf16[16,2048]{1,0:T(8,128)(2,1)S(1)}, bf16[16,2048]{1,0:T(8,128)(2,1)S(1)}, u32[]{:S(2)}, u32[]{:S(2)}) collective-permute-start(bf16[16,2048]{1,0:T(8,128)(2,1)S(1)} %collective-permute-done.5), channel_id=1, source_target_pairs={{1,0},{2,1},{3,2},{4,3},{5,4},{6,5},{7,6},{0,7},{9,8},{10,9},{11,1... | collective-permute-start | bytes 196616 | tf_op jit(solution)/shard_map/ppermute | solution.py:170
  90.2 23.6 %collective-permute-start.8 = (bf16[16,2048]{1,0:T(8,128)(2,1)S(1)}, bf16[16,2048]{1,0:T(8,128)(2,1)}, u32[]{:S(2)}, u32[]{:S(2)}) collective-permute-start(bf16[16,2048]{1,0:T(8,128)(2,1)S(1)} %collective-permute-done.6), channel_id=1, source_target_pairs={{7,0},{0,1},{1,2},{2,3},{3,4},{4,5},{5,6},{6,7},{15,8},{8,9},{9,10... | collective-permute-start | bytes 196616 | tf_op jit(solution)/shard_map/ppermute | solution.py:170
  92.1 19.3 %collective-permute-start.9 = (bf16[8,2048]{1,0:T(8,128)(2,1)S(1)}, bf16[8,2048]{1,0:T(8,128)(2,1)S(1)}, u32[]{:S(2)}, u32[]{:S(2)}) collective-permute-start(bf16[8,2048]{1,0:T(8,128)(2,1)S(1)} %slice.6), channel_id=1, source_target_pairs={{2,0},{3,1},{4,2},{5,3},{6,4},{7,5},{0,6},{1,7},{10,8},{11,9},{12,... | collective-permute-start | bytes 98312 | tf_op jit(solution)/shard_map/ppermute | solution.py:170
  96.4 16.8 %collective-permute-start.10 = (bf16[8,2048]{1,0:T(8,128)(2,1)S(1)}, bf16[8,2048]{1,0:T(8,128)(2,1)S(1)}, u32[]{:S(2)}, u32[]{:S(2)}) collective-permute-start(bf16[8,2048]{1,0:T(8,128)(2,1)S(1)} %slice.7), channel_id=1, source_target_pairs={{6,0},{7,1},{0,2},{1,3},{2,4},{3,5},{4,6},{5,7},{14,8},{15,9},{8,1... | collective-permute-start | bytes 98312 | tf_op jit(solution)/shard_map/ppermute | solution.py:170
  98.3 17.5 %copy-start.5 = (bf16[128,2048]{1,0:T(8,128)(2,1)}, bf16[128,2048]{1,0:T(8,128)(2,1)S(1)}, u32[]{:S(2)}) copy-start(bf16[128,2048]{1,0:T(8,128)(2,1)S(1)} %constant_dynamic-update-slice_fusion.6) | copy-start | bytes 1572868
  113.2 0.6 copy-start.7
  113.8 6.0 %copy-start.8 = (bf16[16,2048]{1,0:T(8,128)(2,1)S(1)}, bf16[16,2048]{1,0:T(8,128)(2,1)}, u32[]{:S(2)}) copy-start(bf16[16,2048]{1,0:T(8,128)(2,1)} %copy-done.7) | copy-start | bytes 196612
  115.8 16.5 %copy-start.6 = (f32[16,2048]{1,0:T(8,128)S(1)}, f32[16,2048]{1,0:T(8,128)}, u32[]{:S(2)}) copy-start(f32[16,2048]{1,0:T(8,128)} %get-tuple-element.33) | copy-start | bytes 393220
  115.8 16.4 %all-to-all-start.3 = ((bf16[8,16,2048]{2,1,0:T(8,128)(2,1)}), bf16[8,16,2048]{2,1,0:T(8,128)(2,1)S(1)}, u32[]{:S(2)}, u32[]{:S(2)}) async-start(bf16[8,16,2048]{2,1,0:T(8,128)(2,1)} %bitcast.35), calls=%async_computation.3 | async-start | bytes 1048576 | tf_op jit(solution)/shard_map/all_to_all | solution.py:36

commit v4 on v3

--- a/solution.py
+++ b/solution.py
@@ -68,22 +68,25 @@
     valid = jnp.logical_and(offset >= 0, offset < lengths)
     bias = jnp.concatenate([jnp.where(valid, 0.0, -1e30)] * group, axis=0)
     square = jnp.zeros((count, HD), jnp.float32)
+    heads = []
     for head in range(KVH):
         lanes = [slice((head * group + h) * HD, (head * group + h + 1) * HD) for h in range(group)]
         query = jnp.concatenate([q_ref[:, lane] for lane in lanes], axis=0)
         own_lane = slice(head * HD, (head + 1) * HD)
         keys = keys_ref[:, :, own_lane].reshape(count * span, HD)
-        values = values_ref[:, :, own_lane].reshape(count * span, HD)
         cached = lax.dot_general(
             query, keys, (((1,), (1,)), ((), ())), preferred_element_type=jnp.float32
         )
         cached = cached * scale + bias
         new_key = jnp.concatenate([new_key_ref[:, own_lane]] * group, axis=0).astype(jnp.float32)
         own = jnp.sum(query.astype(jnp.float32) * new_key, axis=-1, keepdims=True) * scale
-        top = jnp.maximum(jnp.max(cached, axis=-1, keepdims=True), own)
-        weight = jnp.exp(cached - top)
-        own_weight = jnp.exp(own - top)
-        share = 1.0 / (jnp.sum(weight, axis=-1, keepdims=True) + own_weight)
+        heads.append((lanes, own_lane, cached, own))
+    tops = [jnp.maximum(jnp.max(c, axis=-1, keepdims=True), o) for _, _, c, o in heads]
+    weights = [jnp.exp(c - t) for (_, _, c, _), t in zip(heads, tops)]
+    owns = [jnp.exp(o - t) for (_, _, _, o), t in zip(heads, tops)]
+    shares = [1.0 / (jnp.sum(w, axis=-1, keepdims=True) + o) for w, o in zip(weights, owns)]
+    for (lanes, own_lane, _, _), weight, own_weight, share in zip(heads, weights, owns, shares):
+        values = values_ref[:, :, own_lane].reshape(count * span, HD)
         probs = (weight * share).astype(jnp.bfloat16)
         own_prob = (own_weight * share).astype(jnp.bfloat16).astype(jnp.float32)
         mixed = jnp.dot(probs, values, preferred_element_type=jnp.float32)
@@ -280,23 +283,20 @@
     )(*weights)
 
 
-def expert_kernel(x_ref, packed_ref, o_ref, out_ref, sems):
+def expert_kernel(x_ref, packed_ref, o_ref, active_ref, out_ref, sems):
     units = packed_ref.shape[0] // 3
-    both = lax.dot_general(
-        x_ref[...],
-        packed_ref[: 2 * units],
-        (((1,), (1,)), ((), ())),
-        preferred_element_type=jnp.float32,
-    )
-    gated, raised = both[:, :units], both[:, units:]
-    active = (gated / (1.0 + jnp.exp(-gated)) * raised).astype(jnp.bfloat16)
+    across = (((1,), (1,)), ((), ()))
+    x = x_ref[...]
+    gate, up = packed_ref[:units], packed_ref[units : 2 * units]
+    gated = lax.dot_general(x, gate, across, preferred_element_type=jnp.float32)
+    raised = lax.dot_general(x, up, across, preferred_element_type=jnp.float32)
+    active_ref[...] = (gated / (1.0 + jnp.exp(-gated)) * raised).astype(jnp.bfloat16)
     parts, _, part = out_ref.shape
     copies = []
     for i in range(parts):
         lanes = pl.ds(i * part, part)
-        out = jnp.dot(
-            active, packed_ref[2 * units :, lanes], preferred_element_type=jnp.float32
-        )
+        down = packed_ref[2 * units :, lanes]
+        out = jnp.dot(active_ref[...], down, preferred_element_type=jnp.float32)
         out_ref[i] = out.astype(jnp.bfloat16)
         copies.append(pltpu.make_async_copy(out_ref.at[i], o_ref.at[:, lanes], sems.at[i]))
         copies[-1].start()
@@ -314,6 +314,7 @@
         out_specs=pl.BlockSpec(memory_space=pltpu.HBM),
         out_shape=pltpu.HBM((count, width), jnp.bfloat16),
         scratch_shapes=[
+            pltpu.VMEM((count, units), jnp.bfloat16),
             pltpu.VMEM((parts, count, width // parts), jnp.bfloat16),
             pltpu.SemaphoreType.DMA((parts,)),
         ],

time: 135 us -> 134 us (level)
  Pallas kernels: 14.2 us -> 12.7 us
where the time goes in v4:
time: 134 us; the launch traced here: 131 us
  starting transfers between devices  64.6 us (48%)
  waiting for transfers between devices  36.5 us (27%)
  Pallas kernels  12.7 us (9%)
  local copies, waits for them, and re-layouts  12.6 us (9%)
  matrix products  2.58 us (2%)
  other arithmetic  1.53 us (1%)
    all_to_all x4, starting transfers between devices, exchange(): lax.all_to_all(blocks, AXES, split_axis=0, concat_axis=0, axis_index_grou...  30.5 us
    ppermute x8, waiting for transfers between devices, from_row(): lax.ppermute(values, 'tk', [((y + ahead) % NY, y) for y in range(NY)])  27.1 us
    ppermute x8, starting transfers between devices, from_row(): lax.ppermute(values, 'tk', [((y + ahead) % NY, y) for y in range(NY)])  24.7 us
    unnamed x26, local copies, waits for them, and re-layouts  12 us
    ppermute x3, starting transfers between devices, per_device(): lax.ppermute(w, 'rep', [(r, r ^ 1) for r in range(2 * NZH)])  9.43 us
    all_to_all x4, waiting for transfers between devices, exchange(): lax.all_to_all(blocks, AXES, split_axis=0, concat_axis=0, axis_index_grou...  9.41 us
    pallas_call x1, Pallas kernels, expert_apply(): pl.pallas_call(expert_kernel, in_specs=[pl.BlockSpec(memory_space=pltpu.V...  4.33 us
    pallas_call x1, Pallas kernels, attend(): pl.pallas_call(attend_kernel, grid=(1,), in_specs=[pl.BlockSpec(memory_sp...  3.61 us
  transfers between devices with their start and end apart: 15, of which 8 were waited for; matrix products, arithmetic and copies ran while one was open for 6% of the time, Pallas kernels for 2%

profile of v4, /device:TPU:1, one launch (start us, length us, event | category | flops | bytes accessed | tf_op | source)
XLA Modules:
  0.0 131.4 jit_solution(10420496651175419072)
XLA Ops:
  0.7 3.6 %attend.1 = (bf16[8,16,2176]{2,1,0:T(8,128)(2,1)}, f32[16,2048]{1,0:T(8,128)}, bf16[16,2048]{1,0:T(8,128)(2,1)}) custom-call(s32[16]{0:T(128)} %lengths_ref.1, bf16[16,2048]{1,0:T(8,128)(2,1)} %hidden_ref.1, bf16[16,2048]{1,0:T(8,128)(2,1)} %q_ref.1, bf16[16,512]{1,0:T(8,128)(2,1)} %new_key_ref.1, bf16[16,512]{1,0:T(8,128)(2,1)} %new_value_ref.1, ...), custom_call_target="tpu_custom_call" | custom-call | tf_op jit(solution)/shard_map/attend/pallas_call | solution.py:152
  4.3 10.9 %all-to-all-start = ((bf16[8,16,2176]{2,1,0:T(8,128)(2,1)}), bf16[8,16,2176]{2,1,0:T(8,128)(2,1)S(1)}, u32[]{:S(2)}, u32[]{:S(2)}) async-start(bf16[8,16,2176]{2,1,0:T(8,128)(2,1)} %get-tuple-element.34), calls=%async_computation | async-start | bytes 1114112 | tf_op jit(solution)/shard_map/all_to_all | solution.py:36
  15.1 5.1 %collective-permute-start = (bf16[16,2048]{1,0:T(8,128)(2,1)}, bf16[16,2048]{1,0:T(8,128)(2,1)}, u32[]{:S(2)}, u32[]{:S(2)}) collective-permute-start(bf16[16,2048]{1,0:T(8,128)(2,1)} %get-tuple-element.35), channel_id=1, source_target_pairs={{1,0},{2,1},{3,2},{4,3},{5,4},{6,5},{7,6},{0,7},{9,8},{10,9},{11,1... | collective-permute-start | bytes 196616 | tf_op jit(solution)/shard_map/ppermute | solution.py:173
  20.2 1.9 %collective-permute-start.1 = (bf16[16,2048]{1,0:T(8,128)(2,1)}, bf16[16,2048]{1,0:T(8,128)(2,1)S(1)}, u32[]{:S(2)}, u32[]{:S(2)}) collective-permute-start(bf16[16,2048]{1,0:T(8,128)(2,1)} %get-tuple-element.35), channel_id=1, source_target_pairs={{7,0},{0,1},{1,2},{2,3},{3,4},{4,5},{5,6},{6,7},{15,8},{8,9},{9,10... | collective-permute-start | bytes 196616 | tf_op jit(solution)/shard_map/ppermute | solution.py:173
  22.2 2.0 %collective-permute-done = bf16[16,2048]{1,0:T(8,128)(2,1)} collective-permute-done((bf16[16,2048]{1,0:T(8,128)(2,1)}, bf16[16,2048]{1,0:T(8,128)(2,1)}, u32[]{:S(2)}, u32[]{:S(2)}) %collective-permute-start) | collective-permute-done | bytes 65568 | tf_op jit(solution)/shard_map/ppermute | solution.py:173
  24.2 4.2 %collective-permute-done.1 = bf16[16,2048]{1,0:T(8,128)(2,1)S(1)} collective-permute-done((bf16[16,2048]{1,0:T(8,128)(2,1)}, bf16[16,2048]{1,0:T(8,128)(2,1)S(1)}, u32[]{:S(2)}, u32[]{:S(2)}) %collective-permute-start.1) | collective-permute-done | bytes 65568 | tf_op jit(solution)/shard_map/ppermute | solution.py:173
  28.4 2.5 %dispatch.1 = (bf16[512,2048]{1,0:T(8,128)(2,1)}, bf16[128,512]{1,0:T(8,128)(2,1)S(1)}) custom-call(s32[3]{0:T(128)S(1)} %pad_add_fusion.where_ref, bf16[128,2176]{1,0:T(8,128)(2,1)S(1)} %bitcast.24), custom_call_target="tpu_custom_call" | custom-call | tf_op jit(solution)/shard_map/dispatch/pallas_call | solution.py:233
  30.9 8.9 %all-to-all-start.1 = ((bf16[32,16,2048]{2,1,0:T(8,128)(2,1)}), bf16[32,16,2048]{2,1,0:T(8,128)(2,1)S(1)}, u32[]{:S(2)}, u32[]{:S(2)}) async-start(bf16[32,16,2048]{2,1,0:T(8,128)(2,1)} %bitcast.34), calls=%async_computation.1 | async-start | bytes 4194304 | tf_op jit(solution)/shard_map/all_to_all | solution.py:36
  39.9 5.1 %collective-permute-start.2 = (bf16[192,2048]{1,0:T(8,128)(2,1)}, bf16[192,2048]{1,0:T(8,128)(2,1)S(1)}, u32[]{:S(2)}, u32[]{:S(2)}) collective-permute-start(bf16[192,2048]{1,0:T(8,128)(2,1)} %bitcast.26), channel_id=1, source_target_pairs={{0,8},{8,0},{16,24},{24,16},{1,9},{9,1},{17,25},{25,17},{2,10},{10... | collective-permute-start | bytes 2359304 | tf_op jit(solution)/shard_map/ppermute | solution.py:379
  45.0 1.9 %collective-permute-start.3 = (bf16[192,2048]{1,0:T(8,128)(2,1)}, bf16[192,2048]{1,0:T(8,128)(2,1)S(1)}, u32[]{:S(2)}, u32[]{:S(2)}) collective-permute-start(bf16[192,2048]{1,0:T(8,128)(2,1)} %bitcast.28), channel_id=1, source_target_pairs={{0,8},{8,0},{16,24},{24,16},{1,9},{9,1},{17,25},{25,17},{2,10},{10... | collective-permute-start | bytes 2359304 | tf_op jit(solution)/shard_map/ppermute | solution.py:379
  46.9 2.4 %collective-permute-start.4 = (bf16[192,2048]{1,0:T(8,128)(2,1)}, bf16[192,2048]{1,0:T(8,128)(2,1)S(1)}, u32[]{:S(2)}, u32[]{:S(2)}) collective-permute-start(bf16[192,2048]{1,0:T(8,128)(2,1)} %bitcast.30), channel_id=1, source_target_pairs={{0,8},{8,0},{16,24},{24,16},{1,9},{9,1},{17,25},{25,17},{2,10},{10... | collective-permute-start | bytes 2359304 | tf_op jit(solution)/shard_map/ppermute | solution.py:379
  49.3 1.9 %collective-permute-start.5 = (bf16[16,2048]{1,0:T(8,128)(2,1)}, bf16[16,2048]{1,0:T(8,128)(2,1)S(1)}, u32[]{:S(2)}, u32[]{:S(2)}) collective-permute-start(bf16[16,2048]{1,0:T(8,128)(2,1)} %collective-permute-done), channel_id=1, source_target_pairs={{1,0},{2,1},{3,2},{4,3},{5,4},{6,5},{7,6},{0,7},{9,8},{10,9},{11,1... | collective-permute-start | bytes 196616 | tf_op jit(solution)/shard_map/ppermute | solution.py:173
  51.2 3.4 %collective-permute-start.6 = (bf16[16,2048]{1,0:T(8,128)(2,1)S(1)}, bf16[16,2048]{1,0:T(8,128)(2,1)S(1)}, u32[]{:S(2)}, u32[]{:S(2)}) collective-permute-start(bf16[16,2048]{1,0:T(8,128)(2,1)S(1)} %collective-permute-done.1), channel_id=1, source_target_pairs={{7,0},{0,1},{1,2},{2,3},{3,4},{4,5},{5,6},{6,7},{15,8},{8,9},{9,10... | collective-permute-start | bytes 196616 | tf_op jit(solution)/shard_map/ppermute | solution.py:173
  55.8 1.1 copy-done.3
  56.9 1.1 copy-done.4
  58.0 2.2 %pack.1.packed_ref = bf16[1152,2048]{1,0:T(8,128)(2,1)} custom-call(bf16[192,2048]{1,0:T(8,128)(2,1)S(1)} %bitcast.27, bf16[192,2048]{1,0:T(8,128)(2,1)S(1)} %collective-permute-done.2.refs_1_, bf16[192,2048]{1,0:T(8,128)(2,1)S(1)} %bitcast.29, bf16[192,2048]{1,0:T(8,128)(2,1)S(1)} %collective-permute-done.3.refs_3_, bf16[192,2048]{1,0:T(8,128)(2,1)S(1)} %bitcast.31, ...), custom_call_target="tpu_custom_call" | custom-call | bytes 9437184 | tf_op jit(solution)/shard_map/pack/pallas_call | solution.py:272
  60.2 6.1 %collective-permute-done.5 = bf16[16,2048]{1,0:T(8,128)(2,1)S(1)} collective-permute-done((bf16[16,2048]{1,0:T(8,128)(2,1)}, bf16[16,2048]{1,0:T(8,128)(2,1)S(1)}, u32[]{:S(2)}, u32[]{:S(2)}) %collective-permute-start.5) | collective-permute-done | bytes 65568 | tf_op jit(solution)/shard_map/ppermute | solution.py:173
  66.3 2.9 %all-to-all-done.1 = bf16[32,16,2048]{2,1,0:T(8,128)(2,1)S(1)} async-done(((bf16[32,16,2048]{2,1,0:T(8,128)(2,1)}), bf16[32,16,2048]{2,1,0:T(8,128)(2,1)S(1)}, u32[]{:S(2)}, u32[]{:S(2)}) %all-to-all-start.1) | async-done | bytes 2097184 | tf_op jit(solution)/shard_map/all_to_all | solution.py:36
  69.2 2.3 %copy-done.1 = bf16[1152,2048]{1,0:T(8,128)(2,1)S(1)} copy-done((bf16[1152,2048]{1,0:T(8,128)(2,1)S(1)}, bf16[1152,2048]{1,0:T(8,128)(2,1)}, u32[]{:S(2)}) %copy-start.1) | copy-done | bytes 4718616
  71.6 4.3 %experts.1 = bf16[512,2048]{1,0:T(8,128)(2,1)} custom-call(bf16[512,2048]{1,0:T(8,128)(2,1)S(1)} %bitcast.25, bf16[1152,2048]{1,0:T(8,128)(2,1)S(1)} %copy-done.1), custom_call_target="tpu_custom_call" | custom-call | flops 2415919104 | bytes 8912896 | tf_op jit(solution)/shard_map/experts/pallas_call | solution.py:311
  75.9 6.7 %all-to-all-start.2 = ((bf16[32,16,2048]{2,1,0:T(8,128)(2,1)}), bf16[32,16,2048]{2,1,0:T(8,128)(2,1)S(1)}, u32[]{:S(2)}, u32[]{:S(2)}) async-start(bf16[32,16,2048]{2,1,0:T(8,128)(2,1)} %bitcast.33), calls=%async_computation.2 | async-start | bytes 4194304 | tf_op jit(solution)/shard_map/all_to_all | solution.py:36
  84.3 4.3 %collective-permute-start.7 = (bf16[16,2048]{1,0:T(8,128)(2,1)S(1)}, bf16[16,2048]{1,0:T(8,128)(2,1)S(1)}, u32[]{:S(2)}, u32[]{:S(2)}) collective-permute-start(bf16[16,2048]{1,0:T(8,128)(2,1)S(1)} %collective-permute-done.5), channel_id=1, source_target_pairs={{1,0},{2,1},{3,2},{4,3},{5,4},{6,5},{7,6},{0,7},{9,8},{10,9},{11,1... | collective-permute-start | bytes 196616 | tf_op jit(solution)/shard_map/ppermute | solution.py:173
  88.6 1.9 %collective-permute-start.8 = (bf16[16,2048]{1,0:T(8,128)(2,1)S(1)}, bf16[16,2048]{1,0:T(8,128)(2,1)}, u32[]{:S(2)}, u32[]{:S(2)}) collective-permute-start(bf16[16,2048]{1,0:T(8,128)(2,1)S(1)} %collective-permute-done.6), channel_id=1, source_target_pairs={{7,0},{0,1},{1,2},{2,3},{3,4},{4,5},{5,6},{6,7},{15,8},{8,9},{9,10... | collective-permute-start | bytes 196616 | tf_op jit(solution)/shard_map/ppermute | solution.py:173
  90.6 4.3 %collective-permute-start.9 = (bf16[8,2048]{1,0:T(8,128)(2,1)S(1)}, bf16[8,2048]{1,0:T(8,128)(2,1)S(1)}, u32[]{:S(2)}, u32[]{:S(2)}) collective-permute-start(bf16[8,2048]{1,0:T(8,128)(2,1)S(1)} %slice.6), channel_id=1, source_target_pairs={{2,0},{3,1},{4,2},{5,3},{6,4},{7,5},{0,6},{1,7},{10,8},{11,9},{12,... | collective-permute-start | bytes 98312 | tf_op jit(solution)/shard_map/ppermute | solution.py:173
  94.9 1.9 %collective-permute-start.10 = (bf16[8,2048]{1,0:T(8,128)(2,1)S(1)}, bf16[8,2048]{1,0:T(8,128)(2,1)S(1)}, u32[]{:S(2)}, u32[]{:S(2)}) collective-permute-start(bf16[8,2048]{1,0:T(8,128)(2,1)S(1)} %slice.7), channel_id=1, source_target_pairs={{6,0},{7,1},{0,2},{1,3},{2,4},{3,5},{4,6},{5,7},{14,8},{15,9},{8,1... | collective-permute-start | bytes 98312 | tf_op jit(solution)/shard_map/ppermute | solution.py:173
  96.8 13.1 %collective-permute-done.9 = bf16[8,2048]{1,0:T(8,128)(2,1)S(1)} collective-permute-done((bf16[8,2048]{1,0:T(8,128)(2,1)S(1)}, bf16[8,2048]{1,0:T(8,128)(2,1)S(1)}, u32[]{:S(2)}, u32[]{:S(2)}) %collective-permute-start.9) | collective-permute-done | bytes 32800 | tf_op jit(solution)/shard_map/ppermute | solution.py:173
  109.9 1.8 %collective-permute-done.10 = bf16[8,2048]{1,0:T(8,128)(2,1)S(1)} collective-permute-done((bf16[8,2048]{1,0:T(8,128)(2,1)S(1)}, bf16[8,2048]{1,0:T(8,128)(2,1)S(1)}, u32[]{:S(2)}, u32[]{:S(2)}) %collective-permute-start.10) | collective-permute-done | bytes 32800 | tf_op jit(solution)/shard_map/ppermute | solution.py:173
  113.0 1.3 convolution_convert_fusion
  114.2 4.0 %all-to-all-start.3 = ((bf16[8,16,2048]{2,1,0:T(8,128)(2,1)}), bf16[8,16,2048]{2,1,0:T(8,128)(2,1)S(1)}, u32[]{:S(2)}, u32[]{:S(2)}) async-start(bf16[8,16,2048]{2,1,0:T(8,128)(2,1)} %bitcast.35), calls=%async_computation.3 | async-start | bytes 1048576 | tf_op jit(solution)/shard_map/all_to_all | solution.py:36
  120.1 1.5 %constant_dynamic-update-slice_fusion.2 = bf16[128,2048]{1,0:T(8,128)(2,1)} fusion(bf16[128,2048]{1,0:T(8,128)(2,1)} %constant_dynamic-update-slice_fusion.3, bf16[16,2048]{1,0:T(8,128)(2,1)} %collective-permute-done.8), kind=kLoop, calls=%fused_computation.9 | loop fusion | bytes 131072
  122.8 1.3 %convolution_convert_fusion.1 = bf16[128,128]{1,0:T(8,128)(2,1)S(1)} fusion(bf16[128,2048]{1,0:T(8,128)(2,1)} %constant_dynamic-update-slice_fusion, bf16[2048,128]{1,0:T(8,128)(2,1)S(1)} %copy-done), kind=kOutput, calls=%fused_computation.1 | convolution fusion | flops 67125248 | bytes 1081344 | tf_op jit(solution)/shard_map/dot_general | solution.py:400
  124.9 5.8 %all-to-all-done.3 = bf16[8,16,2048]{2,1,0:T(8,128)(2,1)S(1)} async-done(((bf16[8,16,2048]{2,1,0:T(8,128)(2,1)}), bf16[8,16,2048]{2,1,0:T(8,128)(2,1)S(1)}, u32[]{:S(2)}, u32[]{:S(2)}) %all-to-all-start.3) | async-done | bytes 524320 | tf_op jit(solution)/shard_map/all_to_all | solution.py:36
  (37 shorter events, 8.8 us)
Async XLA Ops:
  0.6 122.2 %copy-start = (bf16[2048,128]{1,0:T(8,128)(2,1)S(1)}, bf16[2048,128]{1,0:T(8,128)(2,1)}, u32[]{:S(2)}) copy-start(bf16[2048,128]{1,0:T(8,128)(2,1)} %param.31) | copy-start | bytes 1572868
  4.3 24.1 %all-to-all-start = ((bf16[8,16,2176]{2,1,0:T(8,128)(2,1)}), bf16[8,16,2176]{2,1,0:T(8,128)(2,1)S(1)}, u32[]{:S(2)}, u32[]{:S(2)}) async-start(bf16[8,16,2176]{2,1,0:T(8,128)(2,1)} %get-tuple-element.34), calls=%async_computation | async-start | bytes 1114112 | tf_op jit(solution)/shard_map/all_to_all | solution.py:36
  15.1 9.1 %collective-permute-start = (bf16[16,2048]{1,0:T(8,128)(2,1)}, bf16[16,2048]{1,0:T(8,128)(2,1)}, u32[]{:S(2)}, u32[]{:S(2)}) collective-permute-start(bf16[16,2048]{1,0:T(8,128)(2,1)} %get-tuple-element.35), channel_id=1, source_target_pairs={{1,0},{2,1},{3,2},{4,3},{5,4},{6,5},{7,6},{0,7},{9,8},{10,9},{11,1... | collective-permute-start | bytes 196616 | tf_op jit(solution)/shard_map/ppermute | solution.py:173
  20.2 8.2 %collective-permute-start.1 = (bf16[16,2048]{1,0:T(8,128)(2,1)}, bf16[16,2048]{1,0:T(8,128)(2,1)S(1)}, u32[]{:S(2)}, u32[]{:S(2)}) collective-permute-start(bf16[16,2048]{1,0:T(8,128)(2,1)} %get-tuple-element.35), channel_id=1, source_target_pairs={{7,0},{0,1},{1,2},{2,3},{3,4},{4,5},{5,6},{6,7},{15,8},{8,9},{9,10... | collective-permute-start | bytes 196616 | tf_op jit(solution)/shard_map/ppermute | solution.py:173
  30.9 38.3 %all-to-all-start.1 = ((bf16[32,16,2048]{2,1,0:T(8,128)(2,1)}), bf16[32,16,2048]{2,1,0:T(8,128)(2,1)S(1)}, u32[]{:S(2)}, u32[]{:S(2)}) async-start(bf16[32,16,2048]{2,1,0:T(8,128)(2,1)} %bitcast.34), calls=%async_computation.1 | async-start | bytes 4194304 | tf_op jit(solution)/shard_map/all_to_all | solution.py:36
  39.9 14.8 %collective-permute-start.2 = (bf16[192,2048]{1,0:T(8,128)(2,1)}, bf16[192,2048]{1,0:T(8,128)(2,1)S(1)}, u32[]{:S(2)}, u32[]{:S(2)}) collective-permute-start(bf16[192,2048]{1,0:T(8,128)(2,1)} %bitcast.26), channel_id=1, source_target_pairs={{0,8},{8,0},{16,24},{24,16},{1,9},{9,1},{17,25},{25,17},{2,10},{10... | collective-permute-start | bytes 2359304 | tf_op jit(solution)/shard_map/ppermute | solution.py:379
  45.0 9.7 %collective-permute-start.3 = (bf16[192,2048]{1,0:T(8,128)(2,1)}, bf16[192,2048]{1,0:T(8,128)(2,1)S(1)}, u32[]{:S(2)}, u32[]{:S(2)}) collective-permute-start(bf16[192,2048]{1,0:T(8,128)(2,1)} %bitcast.28), channel_id=1, source_target_pairs={{0,8},{8,0},{16,24},{24,16},{1,9},{9,1},{17,25},{25,17},{2,10},{10... | collective-permute-start | bytes 2359304 | tf_op jit(solution)/shard_map/ppermute | solution.py:379
  46.9 7.7 %collective-permute-start.4 = (bf16[192,2048]{1,0:T(8,128)(2,1)}, bf16[192,2048]{1,0:T(8,128)(2,1)S(1)}, u32[]{:S(2)}, u32[]{:S(2)}) collective-permute-start(bf16[192,2048]{1,0:T(8,128)(2,1)} %bitcast.30), channel_id=1, source_target_pairs={{0,8},{8,0},{16,24},{24,16},{1,9},{9,1},{17,25},{25,17},{2,10},{10... | collective-permute-start | bytes 2359304 | tf_op jit(solution)/shard_map/ppermute | solution.py:379
  49.3 17.0 %collective-permute-start.5 = (bf16[16,2048]{1,0:T(8,128)(2,1)}, bf16[16,2048]{1,0:T(8,128)(2,1)S(1)}, u32[]{:S(2)}, u32[]{:S(2)}) collective-permute-start(bf16[16,2048]{1,0:T(8,128)(2,1)} %collective-permute-done), channel_id=1, source_target_pairs={{1,0},{2,1},{3,2},{4,3},{5,4},{6,5},{7,6},{0,7},{9,8},{10,9},{11,1... | collective-permute-start | bytes 196616 | tf_op jit(solution)/shard_map/ppermute | solution.py:173
  51.2 15.1 %collective-permute-start.6 = (bf16[16,2048]{1,0:T(8,128)(2,1)S(1)}, bf16[16,2048]{1,0:T(8,128)(2,1)S(1)}, u32[]{:S(2)}, u32[]{:S(2)}) collective-permute-start(bf16[16,2048]{1,0:T(8,128)(2,1)S(1)} %collective-permute-done.1), channel_id=1, source_target_pairs={{7,0},{0,1},{1,2},{2,3},{3,4},{4,5},{5,6},{6,7},{15,8},{8,9},{9,10... | collective-permute-start | bytes 196616 | tf_op jit(solution)/shard_map/ppermute | solution.py:173
  54.6 1.1 copy-start.2
  55.8 1.1 copy-start.3
  56.9 1.1 copy-start.4
  69.2 2.3 %copy-start.1 = (bf16[1152,2048]{1,0:T(8,128)(2,1)S(1)}, bf16[1152,2048]{1,0:T(8,128)(2,1)}, u32[]{:S(2)}) copy-start(bf16[1152,2048]{1,0:T(8,128)(2,1)} %pack.1.packed_ref) | copy-start | bytes 14155780
  75.9 37.1 %all-to-all-start.2 = ((bf16[32,16,2048]{2,1,0:T(8,128)(2,1)}), bf16[32,16,2048]{2,1,0:T(8,128)(2,1)S(1)}, u32[]{:S(2)}, u32[]{:S(2)}) async-start(bf16[32,16,2048]{2,1,0:T(8,128)(2,1)} %bitcast.33), calls=%async_computation.2 | async-start | bytes 4194304 | tf_op jit(solution)/shard_map/all_to_all | solution.py:36
  84.3 27.4 %collective-permute-start.7 = (bf16[16,2048]{1,0:T(8,128)(2,1)S(1)}, bf16[16,2048]{1,0:T(8,128)(2,1)S(1)}, u32[]{:S(2)}, u32[]{:S(2)}) collective-permute-start(bf16[16,2048]{1,0:T(8,128)(2,1)S(1)} %collective-permute-done.5), channel_id=1, source_target_pairs={{1,0},{2,1},{3,2},{4,3},{5,4},{6,5},{7,6},{0,7},{9,8},{10,9},{11,1... | collective-permute-start | bytes 196616 | tf_op jit(solution)/shard_map/ppermute | solution.py:173
  88.6 23.6 %collective-permute-start.8 = (bf16[16,2048]{1,0:T(8,128)(2,1)S(1)}, bf16[16,2048]{1,0:T(8,128)(2,1)}, u32[]{:S(2)}, u32[]{:S(2)}) collective-permute-start(bf16[16,2048]{1,0:T(8,128)(2,1)S(1)} %collective-permute-done.6), channel_id=1, source_target_pairs={{7,0},{0,1},{1,2},{2,3},{3,4},{4,5},{5,6},{6,7},{15,8},{8,9},{9,10... | collective-permute-start | bytes 196616 | tf_op jit(solution)/shard_map/ppermute | solution.py:173
  90.6 19.3 %collective-permute-start.9 = (bf16[8,2048]{1,0:T(8,128)(2,1)S(1)}, bf16[8,2048]{1,0:T(8,128)(2,1)S(1)}, u32[]{:S(2)}, u32[]{:S(2)}) collective-permute-start(bf16[8,2048]{1,0:T(8,128)(2,1)S(1)} %slice.6), channel_id=1, source_target_pairs={{2,0},{3,1},{4,2},{5,3},{6,4},{7,5},{0,6},{1,7},{10,8},{11,9},{12,... | collective-permute-start | bytes 98312 | tf_op jit(solution)/shard_map/ppermute | solution.py:173
  94.9 16.8 %collective-permute-start.10 = (bf16[8,2048]{1,0:T(8,128)(2,1)S(1)}, bf16[8,2048]{1,0:T(8,128)(2,1)S(1)}, u32[]{:S(2)}, u32[]{:S(2)}) collective-permute-start(bf16[8,2048]{1,0:T(8,128)(2,1)S(1)} %slice.7), channel_id=1, source_target_pairs={{6,0},{7,1},{0,2},{1,3},{2,4},{3,5},{4,6},{5,7},{14,8},{15,9},{8,1... | collective-permute-start | bytes 98312 | tf_op jit(solution)/shard_map/ppermute | solution.py:173
  96.8 17.4 %copy-start.5 = (bf16[128,2048]{1,0:T(8,128)(2,1)}, bf16[128,2048]{1,0:T(8,128)(2,1)S(1)}, u32[]{:S(2)}) copy-start(bf16[128,2048]{1,0:T(8,128)(2,1)S(1)} %constant_dynamic-update-slice_fusion.6) | copy-start | bytes 1572868
  111.7 0.6 copy-start.7
  112.3 6.0 %copy-start.8 = (bf16[16,2048]{1,0:T(8,128)(2,1)S(1)}, bf16[16,2048]{1,0:T(8,128)(2,1)}, u32[]{:S(2)}) copy-start(bf16[16,2048]{1,0:T(8,128)(2,1)} %copy-done.7) | copy-start | bytes 196612
  114.2 16.5 %copy-start.6 = (f32[16,2048]{1,0:T(8,128)S(1)}, f32[16,2048]{1,0:T(8,128)}, u32[]{:S(2)}) copy-start(f32[16,2048]{1,0:T(8,128)} %get-tuple-element.33) | copy-start | bytes 393220
  114.2 16.5 %all-to-all-start.3 = ((bf16[8,16,2048]{2,1,0:T(8,128)(2,1)}), bf16[8,16,2048]{2,1,0:T(8,128)(2,1)S(1)}, u32[]{:S(2)}, u32[]{:S(2)}) async-start(bf16[8,16,2048]{2,1,0:T(8,128)(2,1)} %bitcast.35), calls=%async_computation.3 | async-start | bytes 1048576 | tf_op jit(solution)/shard_map/all_to_all | solution.py:36

commit v5 on v4

--- a/solution.py
+++ b/solution.py
@@ -370,7 +370,6 @@
 
     near = [from_row(talker_rows, 1), from_row(talker_rows, -1)]
     held = exchange(sent, lines).reshape(line * count, width + experts)
-    held, near = lax.optimization_barrier((held, near))
     slots = 2 * line
     outgoing, weight = dispatch(held, width, slots)
 
@@ -380,7 +379,7 @@
     second = [from_row(near[0], 1), from_row(near[1], -1)]
     arrived = exchange(outgoing.reshape(-1, slots, width), planes).reshape(-1, width)
     packed = pack([own[0], other[0], own[1], other[1], own[2], other[2]])
-    arrived, packed, second = lax.optimization_barrier((arrived, packed, second))
+    arrived, packed = lax.optimization_barrier((arrived, packed))
     computed = expert_apply(arrived, packed)
 
     computed, second = lax.optimization_barrier((computed, second))
@@ -388,7 +387,6 @@
     half = count // 2
     third += [from_row(second[0][:half], 2), from_row(second[1][half:], -2)]
     returned = exchange(computed.reshape(-1, slots, width), planes).reshape(-1, width)
-    returned, third = lax.optimization_barrier((returned, third))
     partial_rows = jnp.dot(weight, returned, preferred_element_type=jnp.float32)
     partial_rows = partial_rows.astype(jnp.bfloat16)
     partial_rows, third = lax.optimization_barrier((partial_rows, third))

time: 134 us -> 133 us (level)
  waiting for transfers between devices: 36.5 us -> 34.9 us
  local copies, waits for them, and re-layouts: 12.6 us -> 14.1 us
    ppermute x8, waiting for transfers between devices: 27.1 us -> 0.02 us  [from_row(): lax.ppermute(values, 'tk', [((y + ahead) % NY, y) for y in range(NY)])]
    all_to_all x4, waiting for transfers between devices: 9.41 us -> 34.9 us  [exchange(): lax.all_to_all(blocks, AXES, split_axis=0, concat_axis=0, axis_index_grou...]
    unnamed x26 -> x22, local copies, waits for them, and re-layouts: 12 us -> 12.2 us
  transfers between devices with their start and end apart: 15 -> 15, of which waited for: 8 -> 4; matrix products, arithmetic and copies ran while one was open for 6% -> 9% of each run, Pallas kernels for 2% -> 7%
where the time goes in v5:
time: 133 us; the launch traced here: 130 us
  starting transfers between devices  63.6 us (48%)
  waiting for transfers between devices  34.9 us (26%)
  local copies, waits for them, and re-layouts  14.1 us (11%)
  Pallas kernels  12.7 us (10%)
  matrix products  2.58 us (2%)
  other arithmetic  1.53 us (1%)
    all_to_all x4, waiting for transfers between devices, exchange(): lax.all_to_all(blocks, AXES, split_axis=0, concat_axis=0, axis_index_grou...  34.9 us
    all_to_all x4, starting transfers between devices, exchange(): lax.all_to_all(blocks, AXES, split_axis=0, concat_axis=0, axis_index_grou...  29.5 us
    ppermute x8, starting transfers between devices, from_row(): lax.ppermute(values, 'tk', [((y + ahead) % NY, y) for y in range(NY)])  24.7 us
    unnamed x22, local copies, waits for them, and re-layouts  12.2 us
    ppermute x3, starting transfers between devices, per_device(): lax.ppermute(w, 'rep', [(r, r ^ 1) for r in range(2 * NZH)])  9.43 us
    pallas_call x1, Pallas kernels, expert_apply(): pl.pallas_call(expert_kernel, in_specs=[pl.BlockSpec(memory_space=pltpu.V...  4.33 us
    pallas_call x1, Pallas kernels, attend(): pl.pallas_call(attend_kernel, grid=(1,), in_specs=[pl.BlockSpec(memory_sp...  3.6 us
  transfers between devices with their start and end apart: 15, of which 4 were waited for; matrix products, arithmetic and copies ran while one was open for 9% of the time, Pallas kernels for 7%

profile of v5, /device:TPU:1, one launch (start us, length us, event | category | flops | bytes accessed | tf_op | source)
XLA Modules:
  0.0 130.3 jit_solution(1879316001257503202)
XLA Ops:
  0.7 3.6 %attend.1 = (bf16[8,16,2176]{2,1,0:T(8,128)(2,1)}, f32[16,2048]{1,0:T(8,128)}, bf16[16,2048]{1,0:T(8,128)(2,1)}) custom-call(s32[16]{0:T(128)} %lengths_ref.1, bf16[16,2048]{1,0:T(8,128)(2,1)} %hidden_ref.1, bf16[16,2048]{1,0:T(8,128)(2,1)} %q_ref.1, bf16[16,512]{1,0:T(8,128)(2,1)} %new_key_ref.1, bf16[16,512]{1,0:T(8,128)(2,1)} %new_value_ref.1, ...), custom_call_target="tpu_custom_call" | custom-call | tf_op jit(solution)/shard_map/attend/pallas_call | solution.py:152
  4.2 10.9 %all-to-all-start = ((bf16[8,16,2176]{2,1,0:T(8,128)(2,1)}), bf16[8,16,2176]{2,1,0:T(8,128)(2,1)S(1)}, u32[]{:S(2)}, u32[]{:S(2)}) async-start(bf16[8,16,2176]{2,1,0:T(8,128)(2,1)} %get-tuple-element.24), calls=%async_computation | async-start | bytes 1114112 | tf_op jit(solution)/shard_map/all_to_all | solution.py:36
  15.1 5.1 %collective-permute-start = (bf16[16,2048]{1,0:T(8,128)(2,1)}, bf16[16,2048]{1,0:T(8,128)(2,1)}, u32[]{:S(2)}, u32[]{:S(2)}) collective-permute-start(bf16[16,2048]{1,0:T(8,128)(2,1)} %get-tuple-element.27), channel_id=1, source_target_pairs={{1,0},{2,1},{3,2},{4,3},{5,4},{6,5},{7,6},{0,7},{9,8},{10,9},{11,1... | collective-permute-start | bytes 196616 | tf_op jit(solution)/shard_map/ppermute | solution.py:173
  20.2 1.9 %collective-permute-start.1 = (bf16[16,2048]{1,0:T(8,128)(2,1)}, bf16[16,2048]{1,0:T(8,128)(2,1)S(1)}, u32[]{:S(2)}, u32[]{:S(2)}) collective-permute-start(bf16[16,2048]{1,0:T(8,128)(2,1)} %get-tuple-element.27), channel_id=1, source_target_pairs={{7,0},{0,1},{1,2},{2,3},{3,4},{4,5},{5,6},{6,7},{15,8},{8,9},{9,10... | collective-permute-start | bytes 196616 | tf_op jit(solution)/shard_map/ppermute | solution.py:173
  22.2 5.7 %all-to-all-done = bf16[8,16,2176]{2,1,0:T(8,128)(2,1)S(1)} async-done(((bf16[8,16,2176]{2,1,0:T(8,128)(2,1)}), bf16[8,16,2176]{2,1,0:T(8,128)(2,1)S(1)}, u32[]{:S(2)}, u32[]{:S(2)}) %all-to-all-start) | async-done | bytes 557088 | tf_op jit(solution)/shard_map/all_to_all | solution.py:36
  27.9 2.5 %dispatch.1 = (bf16[512,2048]{1,0:T(8,128)(2,1)}, bf16[128,512]{1,0:T(8,128)(2,1)S(1)}) custom-call(s32[3]{0:T(128)S(1)} %pad_add_fusion.where_ref, bf16[128,2176]{1,0:T(8,128)(2,1)S(1)} %bitcast.24), custom_call_target="tpu_custom_call" | custom-call | tf_op jit(solution)/shard_map/dispatch/pallas_call | solution.py:233
  30.5 9.4 %all-to-all-start.1 = ((bf16[32,16,2048]{2,1,0:T(8,128)(2,1)}), bf16[32,16,2048]{2,1,0:T(8,128)(2,1)S(1)}, u32[]{:S(2)}, u32[]{:S(2)}) async-start(bf16[32,16,2048]{2,1,0:T(8,128)(2,1)} %bitcast.34), calls=%async_computation.1 | async-start | bytes 4194304 | tf_op jit(solution)/shard_map/all_to_all | solution.py:36
  39.9 5.1 %collective-permute-start.2 = (bf16[192,2048]{1,0:T(8,128)(2,1)}, bf16[192,2048]{1,0:T(8,128)(2,1)S(1)}, u32[]{:S(2)}, u32[]{:S(2)}) collective-permute-start(bf16[192,2048]{1,0:T(8,128)(2,1)} %bitcast.26), channel_id=1, source_target_pairs={{0,8},{8,0},{16,24},{24,16},{1,9},{9,1},{17,25},{25,17},{2,10},{10... | collective-permute-start | bytes 2359304 | tf_op jit(solution)/shard_map/ppermute | solution.py:378
  45.0 1.9 %collective-permute-start.3 = (bf16[192,2048]{1,0:T(8,128)(2,1)}, bf16[192,2048]{1,0:T(8,128)(2,1)S(1)}, u32[]{:S(2)}, u32[]{:S(2)}) collective-permute-start(bf16[192,2048]{1,0:T(8,128)(2,1)} %bitcast.28), channel_id=1, source_target_pairs={{0,8},{8,0},{16,24},{24,16},{1,9},{9,1},{17,25},{25,17},{2,10},{10... | collective-permute-start | bytes 2359304 | tf_op jit(solution)/shard_map/ppermute | solution.py:378
  46.9 2.4 %collective-permute-start.4 = (bf16[192,2048]{1,0:T(8,128)(2,1)}, bf16[192,2048]{1,0:T(8,128)(2,1)S(1)}, u32[]{:S(2)}, u32[]{:S(2)}) collective-permute-start(bf16[192,2048]{1,0:T(8,128)(2,1)} %bitcast.30), channel_id=1, source_target_pairs={{0,8},{8,0},{16,24},{24,16},{1,9},{9,1},{17,25},{25,17},{2,10},{10... | collective-permute-start | bytes 2359304 | tf_op jit(solution)/shard_map/ppermute | solution.py:378
  49.3 1.9 %collective-permute-start.5 = (bf16[16,2048]{1,0:T(8,128)(2,1)}, bf16[16,2048]{1,0:T(8,128)(2,1)S(1)}, u32[]{:S(2)}, u32[]{:S(2)}) collective-permute-start(bf16[16,2048]{1,0:T(8,128)(2,1)} %collective-permute-done), channel_id=1, source_target_pairs={{1,0},{2,1},{3,2},{4,3},{5,4},{6,5},{7,6},{0,7},{9,8},{10,9},{11,1... | collective-permute-start | bytes 196616 | tf_op jit(solution)/shard_map/ppermute | solution.py:173
  51.3 3.4 %collective-permute-start.6 = (bf16[16,2048]{1,0:T(8,128)(2,1)S(1)}, bf16[16,2048]{1,0:T(8,128)(2,1)S(1)}, u32[]{:S(2)}, u32[]{:S(2)}) collective-permute-start(bf16[16,2048]{1,0:T(8,128)(2,1)S(1)} %collective-permute-done.1), channel_id=1, source_target_pairs={{7,0},{0,1},{1,2},{2,3},{3,4},{4,5},{5,6},{6,7},{15,8},{8,9},{9,10... | collective-permute-start | bytes 196616 | tf_op jit(solution)/shard_map/ppermute | solution.py:173
  54.7 1.1 copy-done.2
  55.8 1.1 copy-done.3
  56.9 1.1 copy-done.4
  58.1 2.2 %pack.1.packed_ref = bf16[1152,2048]{1,0:T(8,128)(2,1)} custom-call(bf16[192,2048]{1,0:T(8,128)(2,1)S(1)} %bitcast.27, bf16[192,2048]{1,0:T(8,128)(2,1)S(1)} %collective-permute-done.2.refs_1_, bf16[192,2048]{1,0:T(8,128)(2,1)S(1)} %bitcast.29, bf16[192,2048]{1,0:T(8,128)(2,1)S(1)} %collective-permute-done.3.refs_3_, bf16[192,2048]{1,0:T(8,128)(2,1)S(1)} %bitcast.31, ...), custom_call_target="tpu_custom_call" | custom-call | bytes 9437184 | tf_op jit(solution)/shard_map/pack/pallas_call | solution.py:272
  60.3 9.4 %all-to-all-done.1 = bf16[32,16,2048]{2,1,0:T(8,128)(2,1)S(1)} async-done(((bf16[32,16,2048]{2,1,0:T(8,128)(2,1)}), bf16[32,16,2048]{2,1,0:T(8,128)(2,1)S(1)}, u32[]{:S(2)}, u32[]{:S(2)}) %all-to-all-start.1) | async-done | bytes 2097184 | tf_op jit(solution)/shard_map/all_to_all | solution.py:36
  69.6 2.3 %copy-done.1 = bf16[1152,2048]{1,0:T(8,128)(2,1)S(1)} copy-done((bf16[1152,2048]{1,0:T(8,128)(2,1)S(1)}, bf16[1152,2048]{1,0:T(8,128)(2,1)}, u32[]{:S(2)}) %copy-start.1) | copy-done | bytes 4718616
  72.0 4.3 %experts.1 = bf16[512,2048]{1,0:T(8,128)(2,1)} custom-call(bf16[512,2048]{1,0:T(8,128)(2,1)S(1)} %bitcast.25, bf16[1152,2048]{1,0:T(8,128)(2,1)S(1)} %copy-done.1), custom_call_target="tpu_custom_call" | custom-call | flops 2415919104 | bytes 8912896 | tf_op jit(solution)/shard_map/experts/pallas_call | solution.py:311
  76.3 5.6 %all-to-all-start.2 = ((bf16[32,16,2048]{2,1,0:T(8,128)(2,1)}), bf16[32,16,2048]{2,1,0:T(8,128)(2,1)S(1)}, u32[]{:S(2)}, u32[]{:S(2)}) async-start(bf16[32,16,2048]{2,1,0:T(8,128)(2,1)} %bitcast.33), calls=%async_computation.2 | async-start | bytes 4194304 | tf_op jit(solution)/shard_map/all_to_all | solution.py:36
  81.9 0.8 constant_dynamic-update-slice_fusion.8
  83.6 4.3 %collective-permute-start.7 = (bf16[16,2048]{1,0:T(8,128)(2,1)S(1)}, bf16[16,2048]{1,0:T(8,128)(2,1)}, u32[]{:S(2)}, u32[]{:S(2)}) collective-permute-start(bf16[16,2048]{1,0:T(8,128)(2,1)S(1)} %collective-permute-done.5), channel_id=1, source_target_pairs={{1,0},{2,1},{3,2},{4,3},{5,4},{6,5},{7,6},{0,7},{9,8},{10,9},{11,1... | collective-permute-start | bytes 196616 | tf_op jit(solution)/shard_map/ppermute | solution.py:173
  88.6 1.9 %collective-permute-start.8 = (bf16[16,2048]{1,0:T(8,128)(2,1)S(1)}, bf16[16,2048]{1,0:T(8,128)(2,1)}, u32[]{:S(2)}, u32[]{:S(2)}) collective-permute-start(bf16[16,2048]{1,0:T(8,128)(2,1)S(1)} %collective-permute-done.6), channel_id=1, source_target_pairs={{7,0},{0,1},{1,2},{2,3},{3,4},{4,5},{5,6},{6,7},{15,8},{8,9},{9,10... | collective-permute-start | bytes 196616 | tf_op jit(solution)/shard_map/ppermute | solution.py:173
  91.1 4.2 %collective-permute-start.9 = (bf16[8,2048]{1,0:T(8,128)(2,1)}, bf16[8,2048]{1,0:T(8,128)(2,1)S(1)}, u32[]{:S(2)}, u32[]{:S(2)}) collective-permute-start(bf16[8,2048]{1,0:T(8,128)(2,1)} %slice.6), channel_id=1, source_target_pairs={{2,0},{3,1},{4,2},{5,3},{6,4},{7,5},{0,6},{1,7},{10,8},{11,9},{12,... | collective-permute-start | bytes 98312 | tf_op jit(solution)/shard_map/ppermute | solution.py:173
  95.4 1.9 %collective-permute-start.10 = (bf16[8,2048]{1,0:T(8,128)(2,1)}, bf16[8,2048]{1,0:T(8,128)(2,1)S(1)}, u32[]{:S(2)}, u32[]{:S(2)}) collective-permute-start(bf16[8,2048]{1,0:T(8,128)(2,1)} %slice.7), channel_id=1, source_target_pairs={{6,0},{7,1},{0,2},{1,3},{2,4},{3,5},{4,6},{5,7},{14,8},{15,9},{8,1... | collective-permute-start | bytes 98312 | tf_op jit(solution)/shard_map/ppermute | solution.py:173
  97.3 15.0 %all-to-all-done.2 = bf16[32,16,2048]{2,1,0:T(8,128)(2,1)S(1)} async-done(((bf16[32,16,2048]{2,1,0:T(8,128)(2,1)}), bf16[32,16,2048]{2,1,0:T(8,128)(2,1)S(1)}, u32[]{:S(2)}, u32[]{:S(2)}) %all-to-all-start.2) | async-done | bytes 2097184 | tf_op jit(solution)/shard_map/all_to_all | solution.py:36
  112.3 1.3 convolution_convert_fusion
  113.6 3.6 %all-to-all-start.3 = ((bf16[8,16,2048]{2,1,0:T(8,128)(2,1)}), bf16[8,16,2048]{2,1,0:T(8,128)(2,1)S(1)}, u32[]{:S(2)}, u32[]{:S(2)}) async-start(bf16[8,16,2048]{2,1,0:T(8,128)(2,1)} %bitcast.35), calls=%async_computation.3 | async-start | bytes 1048576 | tf_op jit(solution)/shard_map/all_to_all | solution.py:36
  117.2 1.5 %constant_dynamic-update-slice_fusion.5 = bf16[128,2048]{1,0:T(8,128)(2,1)} fusion(bf16[128,2048]{1,0:T(8,128)(2,1)} %copy-done.5, bf16[16,2048]{1,0:T(8,128)(2,1)} %collective-permute-done.7), kind=kLoop, calls=%fused_computation.12 | loop fusion | bytes 131072
  119.9 1.5 %constant_dynamic-update-slice_fusion.2 = bf16[128,2048]{1,0:T(8,128)(2,1)} fusion(bf16[128,2048]{1,0:T(8,128)(2,1)} %constant_dynamic-update-slice_fusion.3, bf16[16,2048]{1,0:T(8,128)(2,1)} %collective-permute-done.8), kind=kLoop, calls=%fused_computation.9 | loop fusion | bytes 131072
  122.6 1.3 %convolution_convert_fusion.1 = bf16[128,128]{1,0:T(8,128)(2,1)S(1)} fusion(bf16[128,2048]{1,0:T(8,128)(2,1)} %constant_dynamic-update-slice_fusion, bf16[2048,128]{1,0:T(8,128)(2,1)S(1)} %copy-done), kind=kOutput, calls=%fused_computation.1 | convolution fusion | flops 67125248 | bytes 1081344 | tf_op jit(solution)/shard_map/dot_general | solution.py:398
  124.7 4.9 %all-to-all-done.3 = bf16[8,16,2048]{2,1,0:T(8,128)(2,1)S(1)} async-done(((bf16[8,16,2048]{2,1,0:T(8,128)(2,1)}), bf16[8,16,2048]{2,1,0:T(8,128)(2,1)S(1)}, u32[]{:S(2)}, u32[]{:S(2)}) %all-to-all-start.3) | async-done | bytes 524320 | tf_op jit(solution)/shard_map/all_to_all | solution.py:36
  (33 shorter events, 6.1 us)
Async XLA Ops:
  0.6 122.0 %copy-start = (bf16[2048,128]{1,0:T(8,128)(2,1)S(1)}, bf16[2048,128]{1,0:T(8,128)(2,1)}, u32[]{:S(2)}) copy-start(bf16[2048,128]{1,0:T(8,128)(2,1)} %param.31) | copy-start | bytes 1572868
  4.2 23.7 %all-to-all-start = ((bf16[8,16,2176]{2,1,0:T(8,128)(2,1)}), bf16[8,16,2176]{2,1,0:T(8,128)(2,1)S(1)}, u32[]{:S(2)}, u32[]{:S(2)}) async-start(bf16[8,16,2176]{2,1,0:T(8,128)(2,1)} %get-tuple-element.24), calls=%async_computation | async-start | bytes 1114112 | tf_op jit(solution)/shard_map/all_to_all | solution.py:36
  15.1 15.3 %collective-permute-start = (bf16[16,2048]{1,0:T(8,128)(2,1)}, bf16[16,2048]{1,0:T(8,128)(2,1)}, u32[]{:S(2)}, u32[]{:S(2)}) collective-permute-start(bf16[16,2048]{1,0:T(8,128)(2,1)} %get-tuple-element.27), channel_id=1, source_target_pairs={{1,0},{2,1},{3,2},{4,3},{5,4},{6,5},{7,6},{0,7},{9,8},{10,9},{11,1... | collective-permute-start | bytes 196616 | tf_op jit(solution)/shard_map/ppermute | solution.py:173
  20.2 10.2 %collective-permute-start.1 = (bf16[16,2048]{1,0:T(8,128)(2,1)}, bf16[16,2048]{1,0:T(8,128)(2,1)S(1)}, u32[]{:S(2)}, u32[]{:S(2)}) collective-permute-start(bf16[16,2048]{1,0:T(8,128)(2,1)} %get-tuple-element.27), channel_id=1, source_target_pairs={{7,0},{0,1},{1,2},{2,3},{3,4},{4,5},{5,6},{6,7},{15,8},{8,9},{9,10... | collective-permute-start | bytes 196616 | tf_op jit(solution)/shard_map/ppermute | solution.py:173
  30.5 39.2 %all-to-all-start.1 = ((bf16[32,16,2048]{2,1,0:T(8,128)(2,1)}), bf16[32,16,2048]{2,1,0:T(8,128)(2,1)S(1)}, u32[]{:S(2)}, u32[]{:S(2)}) async-start(bf16[32,16,2048]{2,1,0:T(8,128)(2,1)} %bitcast.34), calls=%async_computation.1 | async-start | bytes 4194304 | tf_op jit(solution)/shard_map/all_to_all | solution.py:36
  39.9 14.8 %collective-permute-start.2 = (bf16[192,2048]{1,0:T(8,128)(2,1)}, bf16[192,2048]{1,0:T(8,128)(2,1)S(1)}, u32[]{:S(2)}, u32[]{:S(2)}) collective-permute-start(bf16[192,2048]{1,0:T(8,128)(2,1)} %bitcast.26), channel_id=1, source_target_pairs={{0,8},{8,0},{16,24},{24,16},{1,9},{9,1},{17,25},{25,17},{2,10},{10... | collective-permute-start | bytes 2359304 | tf_op jit(solution)/shard_map/ppermute | solution.py:378
  45.0 9.7 %collective-permute-start.3 = (bf16[192,2048]{1,0:T(8,128)(2,1)}, bf16[192,2048]{1,0:T(8,128)(2,1)S(1)}, u32[]{:S(2)}, u32[]{:S(2)}) collective-permute-start(bf16[192,2048]{1,0:T(8,128)(2,1)} %bitcast.28), channel_id=1, source_target_pairs={{0,8},{8,0},{16,24},{24,16},{1,9},{9,1},{17,25},{25,17},{2,10},{10... | collective-permute-start | bytes 2359304 | tf_op jit(solution)/shard_map/ppermute | solution.py:378
  46.9 7.7 %collective-permute-start.4 = (bf16[192,2048]{1,0:T(8,128)(2,1)}, bf16[192,2048]{1,0:T(8,128)(2,1)S(1)}, u32[]{:S(2)}, u32[]{:S(2)}) collective-permute-start(bf16[192,2048]{1,0:T(8,128)(2,1)} %bitcast.30), channel_id=1, source_target_pairs={{0,8},{8,0},{16,24},{24,16},{1,9},{9,1},{17,25},{25,17},{2,10},{10... | collective-permute-start | bytes 2359304 | tf_op jit(solution)/shard_map/ppermute | solution.py:378
  49.3 27.0 %collective-permute-start.5 = (bf16[16,2048]{1,0:T(8,128)(2,1)}, bf16[16,2048]{1,0:T(8,128)(2,1)S(1)}, u32[]{:S(2)}, u32[]{:S(2)}) collective-permute-start(bf16[16,2048]{1,0:T(8,128)(2,1)} %collective-permute-done), channel_id=1, source_target_pairs={{1,0},{2,1},{3,2},{4,3},{5,4},{6,5},{7,6},{0,7},{9,8},{10,9},{11,1... | collective-permute-start | bytes 196616 | tf_op jit(solution)/shard_map/ppermute | solution.py:173
  51.3 25.1 %collective-permute-start.6 = (bf16[16,2048]{1,0:T(8,128)(2,1)S(1)}, bf16[16,2048]{1,0:T(8,128)(2,1)S(1)}, u32[]{:S(2)}, u32[]{:S(2)}) collective-permute-start(bf16[16,2048]{1,0:T(8,128)(2,1)S(1)} %collective-permute-done.1), channel_id=1, source_target_pairs={{7,0},{0,1},{1,2},{2,3},{3,4},{4,5},{5,6},{6,7},{15,8},{8,9},{9,10... | collective-permute-start | bytes 196616 | tf_op jit(solution)/shard_map/ppermute | solution.py:173
  54.7 1.1 copy-start.2
  55.8 1.1 copy-start.3
  56.9 1.1 copy-start.4
  69.6 2.3 %copy-start.1 = (bf16[1152,2048]{1,0:T(8,128)(2,1)S(1)}, bf16[1152,2048]{1,0:T(8,128)(2,1)}, u32[]{:S(2)}) copy-start(bf16[1152,2048]{1,0:T(8,128)(2,1)} %pack.1.packed_ref) | copy-start | bytes 14155780
  76.3 35.9 %all-to-all-start.2 = ((bf16[32,16,2048]{2,1,0:T(8,128)(2,1)}), bf16[32,16,2048]{2,1,0:T(8,128)(2,1)S(1)}, u32[]{:S(2)}, u32[]{:S(2)}) async-start(bf16[32,16,2048]{2,1,0:T(8,128)(2,1)} %bitcast.33), calls=%async_computation.2 | async-start | bytes 4194304 | tf_op jit(solution)/shard_map/all_to_all | solution.py:36
  83.6 29.9 %collective-permute-start.7 = (bf16[16,2048]{1,0:T(8,128)(2,1)S(1)}, bf16[16,2048]{1,0:T(8,128)(2,1)}, u32[]{:S(2)}, u32[]{:S(2)}) collective-permute-start(bf16[16,2048]{1,0:T(8,128)(2,1)S(1)} %collective-permute-done.5), channel_id=1, source_target_pairs={{1,0},{2,1},{3,2},{4,3},{5,4},{6,5},{7,6},{0,7},{9,8},{10,9},{11,1... | collective-permute-start | bytes 196616 | tf_op jit(solution)/shard_map/ppermute | solution.py:173
  88.6 25.0 %collective-permute-start.8 = (bf16[16,2048]{1,0:T(8,128)(2,1)S(1)}, bf16[16,2048]{1,0:T(8,128)(2,1)}, u32[]{:S(2)}, u32[]{:S(2)}) collective-permute-start(bf16[16,2048]{1,0:T(8,128)(2,1)S(1)} %collective-permute-done.6), channel_id=1, source_target_pairs={{7,0},{0,1},{1,2},{2,3},{3,4},{4,5},{5,6},{6,7},{15,8},{8,9},{9,10... | collective-permute-start | bytes 196616 | tf_op jit(solution)/shard_map/ppermute | solution.py:173
  91.1 22.4 %collective-permute-start.9 = (bf16[8,2048]{1,0:T(8,128)(2,1)}, bf16[8,2048]{1,0:T(8,128)(2,1)S(1)}, u32[]{:S(2)}, u32[]{:S(2)}) collective-permute-start(bf16[8,2048]{1,0:T(8,128)(2,1)} %slice.6), channel_id=1, source_target_pairs={{2,0},{3,1},{4,2},{5,3},{6,4},{7,5},{0,6},{1,7},{10,8},{11,9},{12,... | collective-permute-start | bytes 98312 | tf_op jit(solution)/shard_map/ppermute | solution.py:173
  95.4 18.2 %collective-permute-start.10 = (bf16[8,2048]{1,0:T(8,128)(2,1)}, bf16[8,2048]{1,0:T(8,128)(2,1)S(1)}, u32[]{:S(2)}, u32[]{:S(2)}) collective-permute-start(bf16[8,2048]{1,0:T(8,128)(2,1)} %slice.7), channel_id=1, source_target_pairs={{6,0},{7,1},{0,2},{1,3},{2,4},{3,5},{4,6},{5,7},{14,8},{15,9},{8,1... | collective-permute-start | bytes 98312 | tf_op jit(solution)/shard_map/ppermute | solution.py:173
  97.3 16.3 %copy-start.5 = (bf16[128,2048]{1,0:T(8,128)(2,1)}, bf16[128,2048]{1,0:T(8,128)(2,1)S(1)}, u32[]{:S(2)}) copy-start(bf16[128,2048]{1,0:T(8,128)(2,1)S(1)} %constant_dynamic-update-slice_fusion.6) | copy-start | bytes 1572868
  113.5 16.1 %copy-start.6 = (f32[16,2048]{1,0:T(8,128)S(1)}, f32[16,2048]{1,0:T(8,128)}, u32[]{:S(2)}) copy-start(f32[16,2048]{1,0:T(8,128)} %get-tuple-element.23) | copy-start | bytes 393220
  113.6 16.0 %all-to-all-start.3 = ((bf16[8,16,2048]{2,1,0:T(8,128)(2,1)}), bf16[8,16,2048]{2,1,0:T(8,128)(2,1)S(1)}, u32[]{:S(2)}, u32[]{:S(2)}) async-start(bf16[8,16,2048]{2,1,0:T(8,128)(2,1)} %bitcast.35), calls=%async_computation.3 | async-start | bytes 1048576 | tf_op jit(solution)/shard_map/all_to_all | solution.py:36
